TPU v7x, 128 devices: a whole 4x4x4 slice. The times are simulated.
128 devices in a mesh: rep: 16 (over y_hi, z, core), tp: 8 (over x, y_lo).
Axes of the slice: x: 4, y: 4 (y_hi: 2, y_lo: 2; y = y_hi * 2 + y_lo), z: 4, core: 2. Of those that a mesh axis runs over, the one named last changes fastest.
Arguments:
- hidden_in: bfloat16 [4, 2048, 5120], P(None, 'rep'), may hold values from -6 to 6
- ln_gain: float32 [5120], replicated, may hold values from 0.1 to 1.9
- q_gain: float32 [128], replicated, may hold values from 0.1 to 1.9
- k_gain: float32 [128], replicated, may hold values from 0.1 to 1.9
- w_query: bfloat16 [5120, 8192], P(('rep', 'tp')), may hold values from -0.09782797 to 0.09782797
- w_key: bfloat16 [5120, 1024], P(('rep', 'tp')), may hold values from -0.09782797 to 0.09782797
- w_value: bfloat16 [5120, 1024], P(('rep', 'tp')), may hold values from -0.09782797 to 0.09782797
- w_out: bfloat16 [8192, 5120], P('tp', 'rep'), may hold values from -0.077339804 to 0.077339804
- cache_keys: bfloat16 [2048, 64, 1024], P('rep', None, 'tp'), may hold values from -300 to 300
- cache_values: bfloat16 [2048, 64, 1024], P('rep', None, 'tp'), may hold values from -6 to 6
- cache_lengths: int32 [2048], P('rep'), may hold values from 1 to 64, as said below
- amax_history: float32 [4, 16], replicated, may hold values from 0.7 to 2.8
- cycle_pos: int32 [4], replicated, may hold values from 0 to 15
Outputs:
- mixed_out: bfloat16 [4, 2048, 5120], P(None, 'rep', 'tp')
- new_history: float32 [4, 16], replicated
Inputs may be any that keep to these rules, and one draw needn't show every extreme that they name: `cache_lengths`: among the 128 sequences of each replica at least one holds exactly 64 cached tokens.
All inputs are finite; a program needn't handle non-finite values.
Results may differ from a plain program's by a relative error of at most 0.0086.
Values may be sent and summed in bfloat16 or wider, within the bound.
A program may use at most 192 MiB of HBM per device.

v0:
```python
import jax
import jax.numpy as jnp
from jax import lax
from jax.sharding import PartitionSpec as P

D = 5120
HEADS = 64
KV_HEADS = 8
HEAD_DIM = 128
STEPS = 4
HIST = 16
WINDOW = 8
Q_WIDTH = 8192


fp8_top = 448.0
rope_base = 1000000.0
norm_eps = 1e-06


def fan_roots():
    return jnp.sqrt(jnp.array([D, D, D, Q_WIDTH], dtype=jnp.float32))


def window_amax(history, cycle_pos):
    slot_index = jnp.arange(HIST, dtype=jnp.int32)
    behind = (cycle_pos[:, None] - 1 - slot_index[None, :]) % HIST
    return jnp.max(jnp.where(behind < WINDOW, history, 0.0), axis=1)


def quantize(weight, factor):
    return jnp.clip(weight.astype(jnp.float32) / factor, -fp8_top, fp8_top).astype(jnp.bfloat16)


def rms_scale(values, gain):
    mean_square = jnp.mean(values * values, axis=-1, keepdims=True)
    return values * lax.rsqrt(mean_square + norm_eps) * gain


def rotate(values, positions):
    half_dim = HEAD_DIM // 2
    inverse = rope_base ** (-(2.0 * jnp.arange(half_dim, dtype=jnp.float32)) / HEAD_DIM)
    angles = positions.astype(jnp.float32)[:, None, None] * inverse
    cosine = jnp.cos(angles)
    sine_part = jnp.sin(angles)
    leading = values[..., :half_dim]
    trailing = values[..., half_dim:]
    return jnp.concatenate(
        [leading * cosine - trailing * sine_part, trailing * cosine + leading * sine_part], axis=-1
    )


def attend(queries, new_keys, new_values, cache_keys, cache_values, cache_lengths):
    row_count = cache_keys.shape[0]
    slot_count = cache_keys.shape[1]
    kv_local = new_keys.shape[1] // HEAD_DIM
    group_size = HEADS // KV_HEADS
    group_queries = queries.reshape(STEPS, row_count, kv_local, group_size, HEAD_DIM).transpose(
        1, 2, 0, 3, 4
    )
    group_queries = group_queries.reshape(row_count, kv_local, STEPS * group_size, HEAD_DIM)
    fresh_keys = new_keys.reshape(STEPS, row_count, kv_local, HEAD_DIM)
    fresh_values = new_values.reshape(STEPS, row_count, kv_local, HEAD_DIM)
    old_keys = cache_keys.reshape(row_count, slot_count, kv_local, HEAD_DIM)
    old_values = cache_values.reshape(row_count, slot_count, kv_local, HEAD_DIM)
    scaling = HEAD_DIM ** (-0.5)
    score_old = (
        jnp.einsum("rkqd,rckd->rkqc", group_queries, old_keys, preferred_element_type=jnp.float32)
        * scaling
    )
    score_new = (
        jnp.einsum("rkqd,urkd->rkqu", group_queries, fresh_keys, preferred_element_type=jnp.float32)
        * scaling
    )
    live_old = jnp.arange(slot_count, dtype=jnp.int32)[None, :] < cache_lengths[:, None]
    step_of = jnp.arange(STEPS * group_size, dtype=jnp.int32) // group_size
    live_new = jnp.arange(STEPS, dtype=jnp.int32)[None, :] <= step_of[:, None]
    score_old = jnp.where(live_old[:, None, None, :], score_old, -jnp.inf)
    score_new = jnp.where(live_new[None, None, :, :], score_new, -jnp.inf)
    row_top = jnp.maximum(jnp.max(score_old, axis=-1), jnp.max(score_new, axis=-1))
    raised_old = jnp.exp(score_old - row_top[..., None])
    raised_new = jnp.exp(score_new - row_top[..., None])
    denominator = jnp.sum(raised_old, axis=-1) + jnp.sum(raised_new, axis=-1)
    share_old = (raised_old / denominator[..., None]).astype(jnp.bfloat16)
    share_new = (raised_new / denominator[..., None]).astype(jnp.bfloat16)
    result = jnp.einsum(
        "rkqc,rckd->rkqd", share_old, old_values, preferred_element_type=jnp.float32
    )
    result = result + jnp.einsum(
        "rkqu,urkd->rkqd", share_new, fresh_values, preferred_element_type=jnp.float32
    )
    result = result.astype(jnp.bfloat16).reshape(row_count, kv_local, STEPS, group_size, HEAD_DIM)
    return result.transpose(2, 0, 1, 3, 4).reshape(
        STEPS * row_count, kv_local * group_size * HEAD_DIM
    )


def shards(
    hidden_in,
    ln_gain,
    q_gain,
    k_gain,
    w_query,
    w_key,
    w_value,
    w_out,
    cache_keys,
    cache_values,
    cache_lengths,
    amax_history,
    cycle_pos,
):
    rep_count = lax.axis_size("rep")
    tp_count = lax.axis_size("tp")
    roots = fan_roots()
    scales = window_amax(amax_history, cycle_pos) / (fp8_top * roots)
    current = lax.pmax(
        (
            jnp.max(jnp.abs(w_query)).astype(jnp.float32),
            jnp.max(jnp.abs(w_key)).astype(jnp.float32),
            jnp.max(jnp.abs(w_value)).astype(jnp.float32),
            jnp.max(jnp.abs(w_out)).astype(jnp.float32),
        ),
        ("rep", "tp"),
    )
    stacked = jnp.stack([current[0], current[1], current[2], current[3]]) * roots
    slot_index = jnp.arange(HIST, dtype=jnp.int32)
    new_history = jnp.where(
        slot_index[None, :] == cycle_pos[:, None], stacked[:, None], amax_history
    )
    query_shard = quantize(w_query, scales[0])
    key_shard = quantize(w_key, scales[1])
    value_shard = quantize(w_value, scales[2])
    out_shard = quantize(w_out, scales[3])
    row_count = hidden_in.shape[1]
    total_rows = STEPS * row_count
    flat_rows = hidden_in.reshape(total_rows, D)
    normed = rms_scale(flat_rows.astype(jnp.float32), ln_gain).astype(jnp.bfloat16)
    grouped = (
        lax.all_gather(query_shard, "rep", axis=0, tiled=True),
        lax.all_gather(key_shard, "rep", axis=0, tiled=True),
        lax.all_gather(value_shard, "rep", axis=0, tiled=True),
    )
    relaid = (
        lax.all_to_all(grouped[0], "tp", split_axis=1, concat_axis=0, tiled=True),
        lax.all_to_all(grouped[1], "tp", split_axis=1, concat_axis=0, tiled=True),
        lax.all_to_all(grouped[2], "tp", split_axis=1, concat_axis=0, tiled=True),
    )
    block_size = D // (rep_count * tp_count)
    permuted = (
        normed.reshape(total_rows, rep_count, tp_count, block_size)
        .transpose(0, 2, 1, 3)
        .reshape(total_rows, D)
    )
    queries = jnp.dot(permuted, relaid[0], preferred_element_type=jnp.float32)
    new_keys = jnp.dot(permuted, relaid[1], preferred_element_type=jnp.float32)
    new_values = jnp.dot(permuted, relaid[2], preferred_element_type=jnp.float32)
    positions = (cache_lengths[None, :] + jnp.arange(STEPS, dtype=jnp.int32)[:, None]).reshape(
        total_rows
    )
    head_local = queries.shape[1] // HEAD_DIM
    kv_local = new_keys.shape[1] // HEAD_DIM
    queries = rotate(
        rms_scale(queries.reshape(total_rows, head_local, HEAD_DIM), q_gain), positions
    )
    queries = queries.astype(jnp.bfloat16).reshape(total_rows, head_local * HEAD_DIM)
    new_keys = rotate(
        rms_scale(new_keys.reshape(total_rows, kv_local, HEAD_DIM), k_gain), positions
    )
    new_keys = new_keys.astype(jnp.bfloat16).reshape(total_rows, kv_local * HEAD_DIM)
    new_values = (new_values * scales[2]).astype(jnp.bfloat16)
    attended = attend(queries, new_keys, new_values, cache_keys, cache_values, cache_lengths)
    branch = jnp.dot(
        attended,
        lax.all_gather(out_shard, "rep", axis=1, tiled=True),
        preferred_element_type=jnp.float32,
    )
    summed = lax.psum_scatter(branch, "tp", scatter_dimension=1, tiled=True)
    col_width = summed.shape[1]
    residual = lax.dynamic_slice_in_dim(flat_rows, lax.axis_index("tp") * col_width, col_width, 1)
    mixed_out = (residual.astype(jnp.float32) + summed * scales[3]).astype(jnp.bfloat16)
    return (mixed_out.reshape(STEPS, row_count, col_width), new_history)


def solution(mesh):
    placed = (
        P(None, "rep", None),
        P(),
        P(),
        P(),
        P(("rep", "tp"), None),
        P(("rep", "tp"), None),
        P(("rep", "tp"), None),
        P("tp", "rep"),
        P("rep", None, "tp"),
        P("rep", None, "tp"),
        P("rep"),
        P(),
        P(),
    )
    return jax.shard_map(
        shards, mesh=mesh, in_specs=placed, out_specs=(P(None, "rep", "tp"), P()), check_vma=False
    )
```

profile of v0, /device:TPU:1, one launch (start us, length us, event | category | flops | bytes accessed | tf_op | source)
XLA Modules:
  0.0 730.0 jit_solution(1322981631906906624)
XLA Ops:
  7.2 2.0 abs_reduce_fusion.1
  9.3 1.5 abs_reduce_fusion.3
  10.8 1.5 abs_reduce_fusion.2
  12.3 1.8 abs_reduce_fusion
  14.1 0.7 broadcast_add_fusion
  14.7 69.3 %all-reduce = (f32[1]{0:T(128)}, f32[1]{0:T(128)}, f32[1]{0:T(128)}, f32[1]{0:T(128)}) all-reduce(bf16[1]{0:T(256)(128)(2,1)} %bitcast.38, bf16[1]{0:T(256)(128)(2,1)} %bitcast.37, bf16[1]{0:T(256)(128)(2,1)} %bitcast.36, bf16[1]{0:T(256)(128)(2,1)} %bitcast.35), channel_id=1, replica_groups=mesh['rep'=16,'tp'=8] {'rep','tp'}, use_global_device_ids=true, to_apply=%region_16.17 | all-reduce | flops 4 | bytes 24 | tf_op jit(solution)/shard_map/pmax | solution.py:117
  84.0 3.2 maximum_multiply_fusion
  87.2 1.4 fusion.35
  88.6 0.7 multiply.24
  89.3 0.7 fusion.39
  90.0 2.2 clamp_convert_fusion.3
  92.2 2.2 clamp_convert_fusion.2
  94.5 1.7 clamp_convert_fusion.1
  96.3 1.7 clamp_convert_fusion
  98.0 37.3 %all-gather.7.cloned.1.call-done = bf16[640,1024]{1,0:T(8,128)(2,1)} async-done(((bf16[40,1024]{1,0:T(8,128)(2,1)}), bf16[640,1024]{1,0:T(8,128)(2,1)}) %all-gather.7.cloned.1.call-update) | async-done | bytes 1310736 | tf_op jit(solution)/shard_map/all_gather | solution.py:141
  135.3 2.4 copy.79
  137.7 4.0 all-to-all-start.1
  141.7 48.0 %all-gather.9.cloned.1.call-done = bf16[640,1024]{1,0:T(8,128)(2,1)} async-done(((bf16[40,1024]{1,0:T(8,128)(2,1)}), bf16[640,1024]{1,0:T(8,128)(2,1)}) %all-gather.9.cloned.1.call-update) | async-done | bytes 1310736 | tf_op jit(solution)/shard_map/all_gather | solution.py:142
  189.7 2.4 copy.83
  192.1 1.1 copy-done.1
  193.2 4.0 all-to-all-start.2
  197.2 85.8 %all-gather.5.cloned.1.call-done = bf16[640,8192]{1,0:T(8,128)(2,1)} async-done(((bf16[40,8192]{1,0:T(8,128)(2,1)}), bf16[640,8192]{1,0:T(8,128)(2,1)}) %all-gather.5.cloned.1.call-update) | async-done | bytes 10485776 | tf_op jit(solution)/shard_map/all_gather | solution.py:140
  283.0 14.5 %copy.74 = bf16[640,8192]{0,1:T(8,128)(2,1)} copy(bf16[640,8192]{1,0:T(8,128)(2,1)} %all-gather.5.cloned.1.call-done) | data formatting | bytes 20971520 | tf_op jit(solution)/shard_map/all_gather | solution.py:140
  297.5 15.1 %copy.75 = bf16[640,8,1024]{2,0,1:T(8,128)(2,1)} copy(bf16[640,8,1024]{0,2,1:T(8,128)(2,1)} %bitcast.78) | data formatting | bytes 20971520 | tf_op jit(solution)/shard_map/all_to_all | solution.py:145
  312.6 5.1 all-to-all-start
  317.7 0.2 reduce-scatter.2.cloned.1.call-start
  318.0 9.9 %copy.72 = f32[4,128,5120]{1,0,2:T(4,128)} copy(bf16[4,128,5120]{2,1,0:T(8,128)(2,1)} %param.14) | data formatting | bytes 15728640 | tf_op jit(solution)/shard_map/convert_element_type | solution.py:138
  327.9 12.7 %reshape.404 = f32[512,16,8,40]{0,3,2,1:T(8,128)} reshape(f32[4,128,5120]{1,0,2:T(4,128)} %copy.72) | data formatting | bytes 20971520 | tf_op jit(solution)/shard_map/convert_element_type | solution.py:138
  340.7 3.6 multiply_reduce_fusion
  344.3 5.0 fusion
  349.3 2.8 copy.73
  352.1 0.5 iota_compare_fusion.2
  352.7 0.5 copy-done.9
  353.2 1.2 multiply_cosine_fusion.1
  354.4 2.4 copy.80
  356.8 3.9 multiply_reduce_fusion.2
  360.7 0.1 multiply_bitcast_fusion
  360.8 1.2 fusion.24
  362.0 1.5 concatenate.30
  363.5 1.6 copy.81
  365.2 1.5 concatenate.31
  366.6 1.6 copy.82
  368.3 1.5 copy.84
  369.8 5.1 fusion.5
  374.8 86.6 %all-to-all-done = bf16[640,8,1024]{2,0,1:T(8,128)(2,1)} async-done(((bf16[640,8,1024]{2,0,1:T(8,128)(2,1)}), bf16[640,8,1024]{2,0,1:T(8,128)(2,1)}, u32[]{:S(2)}, u32[]{:S(2)}) %all-to-all-start) | async-done | bytes 10485792 | tf_op jit(solution)/shard_map/all_to_all | solution.py:145
  461.4 13.9 %copy.76 = bf16[5120,1024]{0,1:T(8,128)(2,1)} copy(bf16[5120,1024]{1,0:T(8,128)(2,1)} %bitcast.8) | data formatting | bytes 20971520 | tf_op jit(solution)/shard_map/all_to_all | solution.py:145
  475.4 10.1 %multiply_reduce_fusion.1 = (f32[512,8]{0,1:T(8,128)S(1)}, f32[512,8,128]{0,2,1:T(8,128)S(1)}) fusion(bf16[512,5120,1]{0,1,2:T(8,128)(2,1)} %bitcast.83, bf16[8,128,5120]{2,1,0:T(8,128)(2,1)} %bitcast.80), kind=kOutput, calls=%fused_computation.8 | convolution fusion | flops 5369753600 | bytes 17842176 | tf_op jit(solution)/shard_map/dot_general | solution.py:155
  485.5 0.5 multiply_multiply_fusion
  486.0 0.4 copy-done.5
  486.4 0.4 subtract_convert_fusion
  486.8 0.9 concatenate.27
  487.7 0.9 concatenate.28
  488.6 1.9 maximum_bitcast_fusion
  490.6 2.5 copy.78
  493.1 2.0 fusion.40
  495.1 2.9 fusion.1
  498.1 0.2 fusion.18
  498.3 1.3 fusion.2
  499.6 1.9 fusion.6
  501.5 0.6 fusion.3
  502.1 0.2 copy.86
  502.3 12.1 %fusion.7 = f32[512,5120]{1,0:T(8,128)} fusion(bf16[1024,5120]{0,1:T(8,128)(2,1)} %all-gather.11.cloned.1.call-done, bf16[64,8,8,128]{3,2,1,0:T(8,128)(2,1)S(1)} %bitcast.90), kind=kOutput, calls=%fused_computation.20 | convolution fusion | flops 5368709120 | bytes 22020096 | tf_op jit(solution)/shard_map/dot_general | solution.py:173
  514.5 205.8 %reduce-scatter.2.cloned.1.call-done = f32[512,640]{1,0:T(8,128)} async-done(((f32[512,5120]{1,0:T(8,128)}), f32[512,640]{1,0:T(8,128)}) %reduce-scatter.2.cloned.1.call-update) | async-done | bytes 1310736 | tf_op jit(solution)/shard_map/reduce_scatter | solution.py:178
  720.3 3.2 add_convert_fusion.1
  (51 shorter events, 0.6 us)
Async XLA Ops:
  7.2 492.5 %copy-start = (bf16[128,64,128]{2,1,0:T(8,128)(2,1)S(1)}, bf16[128,64,128]{2,1,0:T(8,128)(2,1)}, u32[]{:S(2)}) copy-start(bf16[128,64,128]{2,1,0:T(8,128)(2,1)} %param.23) | copy-start | bytes 6291460
  7.2 87.3 %copy-start.3 = (bf16[40,8192]{1,0:T(8,128)(2,1)S(1)}, bf16[40,8192]{1,0:T(8,128)(2,1)}, u32[]{:S(2)}) copy-start(bf16[40,8192]{1,0:T(8,128)(2,1)} %param.18) | copy-start | bytes 1966084
  7.2 89.1 %copy-start.4 = (bf16[1024,320]{0,1:T(8,128)(2,1)S(1)}, bf16[1024,320]{0,1:T(8,128)(2,1)}, u32[]{:S(2)}) copy-start(bf16[1024,320]{0,1:T(8,128)(2,1)} %param.21) | copy-start | bytes 1966084
  7.2 128.1 %all-gather.7.cloned.1.call-start = ((), (), s32[]{:S(2)}) async-start(), calls=%async_computation.5 | async-start | bytes 1392640 | tf_op jit(solution)/shard_map/all_gather | solution.py:141
  92.2 97.5 %all-gather.9.cloned.1.call-start = ((), (), s32[]{:S(2)}) async-start(), calls=%async_computation.6 | async-start | bytes 1392640 | tf_op jit(solution)/shard_map/all_gather | solution.py:142
  94.4 188.6 %all-gather.5.cloned.1.call-start = ((), (), s32[]{:S(2)}) async-start(), calls=%async_computation.4 | async-start | bytes 11141120 | tf_op jit(solution)/shard_map/all_gather | solution.py:140
  96.2 406.1 %all-gather.11.cloned.1.call-start = ((), (), s32[]{:S(2)}) async-start(), calls=%async_computation.7 | async-start | bytes 11141120 | tf_op jit(solution)/shard_map/all_gather | solution.py:175
  137.7 54.4 %all-to-all-start.1 = ((bf16[640,8,128]{0,2,1:T(8,128)(2,1)}), bf16[640,8,128]{0,2,1:T(8,128)(2,1)S(1)}, u32[]{:S(2)}, u32[]{:S(2)}) async-start(bf16[640,8,128]{0,2,1:T(8,128)(2,1)} %bitcast.87), calls=%async_computation.1 | async-start | bytes 2621440 | tf_op jit(solution)/shard_map/all_to_all | solution.py:146
  192.1 1.1 copy-start.1
  193.2 119.4 %all-to-all-start.2 = ((bf16[640,8,128]{0,2,1:T(8,128)(2,1)}), bf16[640,8,128]{0,2,1:T(8,128)(2,1)S(1)}, u32[]{:S(2)}, u32[]{:S(2)}) async-start(bf16[640,8,128]{0,2,1:T(8,128)(2,1)} %bitcast.86), calls=%async_computation.2 | async-start | bytes 2621440 | tf_op jit(solution)/shard_map/all_to_all | solution.py:147
  312.6 148.8 %all-to-all-start = ((bf16[640,8,1024]{2,0,1:T(8,128)(2,1)}), bf16[640,8,1024]{2,0,1:T(8,128)(2,1)}, u32[]{:S(2)}, u32[]{:S(2)}) async-start(bf16[640,8,1024]{2,0,1:T(8,128)(2,1)} %copy.75), calls=%async_computation | async-start | bytes 20971520 | tf_op jit(solution)/shard_map/all_to_all | solution.py:145
  317.7 402.6 %reduce-scatter.2.cloned.1.call-start = ((), (), s32[]{:S(2)}) async-start(), calls=%async_computation.8 | async-start | bytes 11796480 | tf_op jit(solution)/shard_map/reduce_scatter | solution.py:178
  327.9 12.7 %copy-start.8 = (f32[5120]{0:T(1024)S(1)}, f32[5120]{0:T(1024)}, u32[]{:S(2)}) copy-start(f32[5120]{0:T(1024)} %param.15) | copy-start | bytes 61444
  349.3 3.3 copy-start.13
  352.1 2.3 copy-start.11
  352.6 0.6 copy-start.9
  356.8 3.9 copy-start.14
  356.8 4.0 copy-start.10
  356.8 4.0 copy-start.12
  475.4 10.1 %copy-start.15 = (f32[128]{0:T(128)S(1)}, f32[128]{0:T(128)}, u32[]{:S(2)}) copy-start(f32[128]{0:T(128)} %param.16) | copy-start | bytes 1540
  485.5 0.9 copy-start.5
  488.6 4.4 copy-start.6
  488.6 4.4 copy-start.7
  493.1 2.1 copy-start.2
Sparse Core Ops, SparseCore 0:
  92.3 42.9 all-gather.6
  137.7 51.9 all-gather.8
  192.2 90.7 all-gather.4
  285.9 185.7 all-gather.10
  514.6 205.6 reduce-scatter.1
where the time goes:
time: 733 us; the launch traced here: 730 us
  waiting for transfers between devices  464 us (63%)
  local copies, waits for them, and re-layouts  91.3 us (12%)
  blocking collectives  69.3 us (9%)
  other arithmetic  39.8 us (5%)
  matrix products  38.5 us (5%)
  between operations  14.1 us (2%)
  starting transfers between devices  13.5 us (2%)
    reduce_scatter x1, waiting for transfers between devices, shards(): summed = lax.psum_scatter(branch, 'tp', scatter_dimension=1, tiled=True)  206 us
    all_to_all x1, waiting for transfers between devices, shards(): lax.all_to_all(grouped[0], 'tp', split_axis=1, concat_axis=0, tiled=True)  86.6 us
    all_gather x1, waiting for transfers between devices, shards(): lax.all_gather(query_shard, 'rep', axis=0, tiled=True)  85.8 us
    pmax x1, blocking collectives, shards(): lax.pmax((jnp.max(jnp.abs(w_query)).astype(jnp.float32), jnp.max(jnp.abs(...  69.3 us
    all_gather x1, waiting for transfers between devices, shards(): lax.all_gather(value_shard, 'rep', axis=0, tiled=True)  48 us
    all_gather x1, waiting for transfers between devices, shards(): lax.all_gather(key_shard, 'rep', axis=0, tiled=True)  37.3 us
    all_to_all x2, local copies, waits for them, and re-layouts, shards(): lax.all_to_all(grouped[0], 'tp', split_axis=1, concat_axis=0, tiled=True)  29.1 us
    convert_element_type x2, local copies, waits for them, and re-layouts, shards(): flat_rows.astype(jnp.float32)  22.6 us
  transfers between devices with their start and end apart: 8, of which 5 were waited for; matrix products, arithmetic and copies ran while one was open for 19% of the time, Pallas kernels for 0%

commit v1 on v0

v1 whole, which is shorter than its diff:
```python
import jax
import jax.numpy as jnp
import numpy as np
from jax import lax
from jax.experimental import pallas as pl
from jax.experimental.pallas import tpu as pltpu
from jax.sharding import PartitionSpec as P

D = 5120
HEADS = 64
KV_HEADS = 8
HEAD_DIM = 128
STEPS = 4
HIST = 16
WINDOW = 8
Q_WIDTH = 8192
CACHE = 64
SEQS = 128
ROWS = STEPS * SEQS
REPS = 16
TPS = 8
SPOTS = 8
SHARD = 40
Q_LOCAL = 1024
HALF = 640
PACKED = 80
OUT_SHARD = 320

fp8_top = 448.0
rope_base = 1000000.0
norm_eps = 1e-06

BF = jnp.bfloat16
F32 = jnp.float32
MESH = pl.DeviceIdType.MESH


def spread_matrices():
    place = np.zeros((2, HALF, 768), np.float32)
    for block in range(16):
        for row in range(32):
            place[0, block * SHARD + row, block * 48 + row] = 1.0
            place[1, block * SHARD + row, block * 48 + 16 + row] = 1.0
        for row in range(8):
            place[0, block * SHARD + 32 + row, block * 48 + 32 + row] = 1.0
            place[1, block * SHARD + 32 + row, block * 48 + 8 + row] = 1.0
    return place


def join_matrices():
    place = np.zeros((2, 384, HALF), np.float32)
    for col in range(OUT_SHARD):
        place[0, col, col] = 1.0
        place[1, col, OUT_SHARD + col] = 1.0
    return place


def dot(a, b):
    return jnp.dot(a, b, preferred_element_type=F32)


def quantize(weight, factor):
    return jnp.clip(weight.astype(F32) / factor, -fp8_top, fp8_top)


def kernel(
    hidden,
    ln_gain,
    q_gain,
    k_gain,
    w_query,
    w_key,
    w_value,
    w_out,
    cache_keys,
    cache_values,
    lengths,
    history,
    cycle,
    spread,
    join,
    freq,
    mixed,
    new_history,
    rows_in,
    keys_in,
    values_in,
    stage,
    wbuf,
    obuf,
    oshard,
    oside,
    xp,
    acc,
    att,
    attb,
    rs_send,
    rs_recv,
    resid,
    amax_out,
    amax_in,
    local_sem,
    a2a_s,
    a2a_r,
    w_s,
    w_r,
    o_s,
    o_r,
    side_s,
    side_r,
    rs_s,
    rs_r,
    am_s,
    am_r,
):
    rep = lax.axis_index("rep")
    tp = lax.axis_index("tp")
    yh = rep // 8
    zz = (rep // 2) % 4
    core = rep % 2
    spot = rep // 2

    def rep_of(dy, dz, flip):
        return ((yh + dy) % 2) * 8 + ((zz + dz) % 4) * 2 + (core + flip) % 2

    def spot_of(dy, dz):
        return ((yh + dy) % 2) * 4 + (zz + dz) % 4

    def at_rep(index):
        return {"rep": index, "tp": tp}

    def at_tp(index):
        return {"rep": rep, "tp": index}

    peers = [(tp + s) % TPS for s in range(1, TPS)]
    y_far = rep_of(1, 0, 0)
    z_up = rep_of(0, 1, 0)
    z_down = rep_of(0, 3, 0)
    sibling = rep_of(0, 0, 1)

    loads = []
    for i in range(SPOTS):
        loads.append(
            pltpu.make_async_copy(hidden.at[:, pl.ds(i * HALF, HALF)], rows_in.at[i], local_sem.at[i])
        )
    loads.append(pltpu.make_async_copy(cache_keys, keys_in, local_sem.at[8]))
    loads.append(pltpu.make_async_copy(cache_values, values_in, local_sem.at[9]))
    loads.append(
        pltpu.make_async_copy(
            hidden.at[:, pl.ds(pl.multiple_of(tp * HALF, 128), HALF)], resid, local_sem.at[10]
        )
    )
    for load in loads:
        load.start()

    barrier = pltpu.get_barrier_semaphore()
    for peer in peers:
        pl.semaphore_signal(barrier, inc=1, device_id=at_tp(peer), device_id_type=MESH)
    for other in (y_far, z_up, z_down, sibling):
        pl.semaphore_signal(barrier, inc=1, device_id=at_rep(other), device_id_type=MESH)

    slot = lax.broadcasted_iota(jnp.int32, (1, HIST), 1)
    fans = (D, D, D, Q_WIDTH)
    roots = [float(np.sqrt(np.float32(fan))) for fan in fans]
    scales = []
    for m in range(4):
        behind = jnp.bitwise_and(cycle[m] + (2 * HIST - 1) - slot, HIST - 1)
        limit = jnp.max(
            jnp.where(behind < WINDOW, history[m : m + 1, :], 0.0), axis=1, keepdims=True
        )
        scales.append(limit / (fp8_top * roots[m]))

    def pack(j, tops):
        query = w_query[:, pl.ds(pl.multiple_of(j * Q_LOCAL, 128), Q_LOCAL)]
        key = w_key[:, pl.ds(pl.multiple_of(j * 128, 128), 128)]
        value = w_value[:, pl.ds(pl.multiple_of(j * 128, 128), 128)]
        q0 = quantize(query, scales[0])
        k0 = quantize(key, scales[1])
        v0 = quantize(value, scales[2])
        first = q0[:, :HALF]
        second = jnp.concatenate([q0[:, HALF:], k0, v0], axis=1)
        stage[j, 0:32, :] = first[0:32].astype(BF)
        stage[j, 32:48, :] = jnp.concatenate([first[32:40], second[32:40]], axis=0).astype(BF)
        stage[j, 48:80, :] = second[0:32].astype(BF)

        def top(values, old):
            found = jnp.max(jnp.abs(values.astype(F32)), axis=0, keepdims=True)
            for i in range(values.shape[1] // 128):
                old = jnp.maximum(old, found[:, i * 128 : (i + 1) * 128])
            return old

        return top(query, tops[0]), top(key, tops[1]), top(value, tops[2])

    none = jnp.zeros((1, 128), F32)
    tops = lax.fori_loop(0, TPS, pack, (none, none, none))

    pl.semaphore_wait(barrier, 11)

    a2a = []
    for s, peer in enumerate(peers):
        a2a.append(
            pltpu.make_async_remote_copy(
                src_ref=stage.at[peer],
                dst_ref=wbuf.at[rep, tp],
                send_sem=a2a_s.at[s],
                recv_sem=a2a_r.at[s],
                device_id=at_tp(peer),
                device_id_type=MESH,
            )
        )
    for copy in a2a:
        copy.start()
    own_plane = pltpu.make_async_copy(stage.at[tp], wbuf.at[rep, tp], local_sem.at[11])
    own_plane.start()

    def pack_out(i, old):
        rows = pl.ds(pl.multiple_of(i * 128, 128), 128)
        shard = w_out[rows, :]
        ready = quantize(shard, scales[3])
        oshard[rows, :] = jnp.concatenate([ready, jnp.zeros((128, 64), F32)], axis=1).astype(BF)
        found = jnp.max(jnp.abs(shard.astype(F32)), axis=0, keepdims=True)
        return jnp.maximum(old, jnp.max(found, axis=1, keepdims=True))

    top_out = lax.fori_loop(0, 8, pack_out, jnp.zeros((1, 1), F32))
    side = pltpu.make_async_remote_copy(
        src_ref=oshard.at[pl.ds(pl.multiple_of((1 - core) * 512, 512), 512)],
        dst_ref=oside,
        send_sem=side_s,
        recv_sem=side_r,
        device_id=at_rep(sibling),
        device_id_type=MESH,
    )
    side.start()

    tile_row = lax.broadcasted_iota(jnp.int32, (8, 128), 0)
    found = [jnp.max(top, axis=1, keepdims=True) for top in tops] + [top_out]
    tile = jnp.zeros((8, 128), F32)
    for m in range(4):
        tile = jnp.where(tile_row == m, found[m], tile)
    amax_out[0] = tile

    def send_amax(stage_index, slot_index, where):
        return pltpu.make_async_remote_copy(
            src_ref=amax_out.at[stage_index],
            dst_ref=amax_in.at[slot_index],
            send_sem=am_s.at[slot_index],
            recv_sem=am_r.at[slot_index],
            device_id=where,
            device_id_type=MESH,
        )

    am_tp = [send_amax(0, s, at_tp(peer)) for s, peer in enumerate(peers)]
    am_y = [send_amax(1, 7, at_rep(y_far))]
    am_z = [send_amax(2, 8, at_rep(z_up)), send_amax(2, 9, at_rep(z_down))]
    am_w = [send_amax(3, 10, at_rep(z_up))]
    am_c = [send_amax(4, 11, at_rep(sibling))]

    def fold(copies, index, slots):
        for copy in copies:
            copy.wait()
        total = amax_out[index]
        for where in slots:
            total = jnp.maximum(total, amax_in[where])
        amax_out[index + 1] = total

    for copy in am_tp:
        copy.start()

    for load in loads[:8]:
        load.wait()

    def norm(i, carry):
        rows = pl.ds(pl.multiple_of(i * 32, 32), 32)
        parts = [rows_in[j, rows, :].astype(F32) for j in range(SPOTS)]
        square = parts[0] * parts[0]
        for part in parts[1:]:
            square = square + part * part
        mean = jnp.sum(square, axis=1, keepdims=True) / D
        factor = lax.rsqrt(mean + norm_eps)
        for j in range(SPOTS):
            gain = ln_gain[0:1, j * HALF : (j + 1) * HALF]
            rows_in[j, rows, :] = (parts[j] * factor * gain).astype(BF)
        return carry

    lax.fori_loop(0, ROWS // 32, norm, 0)

    def relay(buf, view, send_sem, recv_sem):
        sent = []

        def send(block, half, target):
            copy = pltpu.make_async_remote_copy(
                src_ref=view(buf, block, half),
                dst_ref=view(buf, block, half),
                send_sem=send_sem.at[len(sent)],
                recv_sem=recv_sem.at[block, half],
                device_id=at_rep(target),
                device_id_type=MESH,
            )
            copy.start()
            sent.append(copy)

        def arrive(block, half):
            pltpu.make_async_remote_copy(
                src_ref=view(buf, block, half),
                dst_ref=view(buf, block, half),
                send_sem=send_sem.at[0],
                recv_sem=recv_sem.at[block, half],
                device_id=at_rep(sibling),
                device_id_type=MESH,
            ).wait_recv()

        return send, arrive, sent

    def view_w(buf, block, half):
        return buf.at[block, pl.ds(half * 4, 4)]

    def view_o(buf, block, half):
        return buf.at[block, pl.ds(half * 256, 256)]

    send_w, arrive_w, sent_w = relay(wbuf, view_w, w_s, w_r)
    send_o, arrive_o, sent_o = relay(obuf, view_o, o_s, o_r)

    def own(send):
        for half in range(2):
            for target in (y_far, z_up, z_down, sibling):
                send(rep, half, target)

    def far(send, arrive):
        for half in range(2):
            arrive(y_far, half)
            for target in (z_up, z_down, sibling):
                send(y_far, half, target)

    def beside(send, arrive, dy, dz):
        block = rep_of(dy, dz, 0)
        target, keep = (z_down, 0) if dz == 1 else (z_up, 1)
        for half in range(2):
            arrive(block, half)
            if half == keep:
                send(block, half, target)
            send(block, half, sibling)

    def across(send, arrive, dy):
        block = rep_of(dy, 2, 0)
        for half in range(2):
            arrive(block, half)
            send(block, half, sibling)

    def from_sibling(arrive, dy, dz):
        block = rep_of(dy, dz, 1)
        for half in range(2):
            arrive(block, half)

    side.wait()
    mine = pl.ds(pl.multiple_of(core * 512, 512), 512)
    obuf[rep] = (dot(oshard[mine, :], join[core]) + dot(oside[...], join[1 - core])).astype(BF)
    own(send_o)

    own_plane.wait()
    for copy in a2a:
        copy.wait()
    own(send_w)

    acc[...] = jnp.zeros_like(acc)

    def project(dy, dz):
        place = spot_of(dy, dz)
        for h in range(2):
            def tiles(i, carry):
                rows = pl.ds(pl.multiple_of(i * 256, 256), 256)
                xs = dot(rows_in[place, rows, :], spread[h]).astype(BF)
                total = acc[h, rows, :]
                for cc in range(2):
                    block = wbuf[place * 2 + cc, :, h * 32 : h * 32 + 48, :].reshape(384, HALF)
                    total = total + dot(xs[:, cc * 384 : (cc + 1) * 384], block)
                acc[h, rows, :] = total
                return carry

            lax.fori_loop(0, 2, tiles, 0)

    from_sibling(arrive_w, 0, 0)
    project(0, 0)
    fold(am_tp, 0, range(7))
    am_y[0].start()
    far(send_w, arrive_w)
    beside(send_w, arrive_w, 0, 1)
    beside(send_w, arrive_w, 0, 3)
    from_sibling(arrive_w, 1, 0)
    project(1, 0)
    fold(am_y, 1, [7])
    for copy in am_z:
        copy.start()
    from_sibling(arrive_w, 0, 1)
    project(0, 1)
    from_sibling(arrive_w, 0, 3)
    project(0, 3)
    fold(am_z, 2, [8, 9])
    am_w[0].start()
    beside(send_w, arrive_w, 1, 1)
    beside(send_w, arrive_w, 1, 3)
    far(send_o, arrive_o)
    beside(send_o, arrive_o, 0, 1)
    beside(send_o, arrive_o, 0, 3)
    from_sibling(arrive_w, 1, 1)
    project(1, 1)
    from_sibling(arrive_w, 1, 3)
    project(1, 3)
    fold(am_w, 3, [10])
    am_c[0].start()
    across(send_w, arrive_w, 0)
    from_sibling(arrive_w, 0, 2)
    project(0, 2)
    across(send_w, arrive_w, 1)
    from_sibling(arrive_w, 1, 2)
    project(1, 2)
    fold(am_c, 4, [11])
    history_row = lax.broadcasted_iota(jnp.int32, (1, HIST), 1)
    for m in range(4):
        new_history[m : m + 1, :] = jnp.where(
            history_row == cycle[m],
            amax_out[5, m : m + 1, 0:1] * roots[m],
            history[m : m + 1, :],
        )

    def head_norm(s, carry):
        rows = pl.ds(pl.multiple_of(s * SEQS, SEQS), SEQS)
        angles = (lengths[...] + s).astype(F32) * freq[...]
        cosine = jnp.cos(angles)
        sine = jnp.sin(angles)
        lane = lax.broadcasted_iota(jnp.int32, (SEQS, HEAD_DIM), 1)
        sine = jnp.where(lane < 64, -sine, sine)
        for head in range(9):
            h, lanes = (0, head) if head < 5 else (1, head - 5)
            cols = pl.ds(lanes * HEAD_DIM, HEAD_DIM)
            values = acc[h, rows, cols]
            gain = q_gain[...] if head < 8 else k_gain[...]
            mean = jnp.sum(values * values, axis=1, keepdims=True) / HEAD_DIM
            values = values * lax.rsqrt(mean + norm_eps) * gain
            acc[h, rows, cols] = values * cosine + pltpu.roll(values, 64, 1) * sine
        cols = pl.ds(512, HEAD_DIM)
        acc[1, rows, cols] = acc[1, rows, cols] * scales[2]
        return carry

    lax.fori_loop(0, STEPS, head_norm, 0)

    for load in loads[8:]:
        load.wait()

    old_seq = lax.broadcasted_iota(jnp.int32, (8, 8 * CACHE), 0)
    old_col = lax.broadcasted_iota(jnp.int32, (8, 8 * CACHE), 1)
    old_slot = jnp.where(
        jnp.right_shift(old_col, 6) == old_seq, jnp.bitwise_and(old_col, CACHE - 1), CACHE
    )
    new_row = lax.broadcasted_iota(jnp.int32, (32, 32), 0)
    new_col = lax.broadcasted_iota(jnp.int32, (32, 32), 1)
    new_live = (jnp.bitwise_and(new_row, 7) == jnp.bitwise_and(new_col, 7)) & (
        jnp.right_shift(new_col, 3) <= jnp.right_shift(new_row, 3)
    )
    new_bias = jnp.where(new_live, 0.0, -1e30)
    scaling = HEAD_DIM ** (-0.5)
    nt = (((1,), (1,)), ((), ()))

    def attend(g, carry):
        first = pl.multiple_of(g * 8, 8)
        seqs = pl.ds(first, 8)

        def pick(h, lanes):
            return [
                acc[h, pl.ds(pl.multiple_of(s * SEQS + g * 8, 8), 8), pl.ds(lanes * HEAD_DIM, HEAD_DIM)]
                for s in range(STEPS)
            ]

        rows = []
        for head in range(8):
            rows += pick(0, head) if head < 5 else pick(1, head - 5)
        queries = jnp.concatenate(rows, axis=0).astype(BF)
        fresh_keys = jnp.concatenate(pick(1, 3), axis=0).astype(BF)
        fresh_values = jnp.concatenate(pick(1, 4), axis=0).astype(BF)
        old_keys = keys_in[seqs].reshape(8 * CACHE, HEAD_DIM)
        old_values = values_in[seqs].reshape(8 * CACHE, HEAD_DIM)
        old_bias = jnp.where(old_slot < lengths[seqs, :], 0.0, -1e30)
        old = lax.dot_general(queries, old_keys, nt, preferred_element_type=F32)
        new = lax.dot_general(queries, fresh_keys, nt, preferred_element_type=F32)
        old = (old.reshape(32, 8, 8 * CACHE) * scaling + old_bias[None]).reshape(256, 8 * CACHE)
        new = (new.reshape(8, 32, 32) * scaling + new_bias[None]).reshape(256, 32)
        top = jnp.maximum(
            jnp.max(old, axis=1, keepdims=True), jnp.max(new, axis=1, keepdims=True)
        )
        old = jnp.exp(old - top)
        new = jnp.exp(new - top)
        total = jnp.sum(old, axis=1, keepdims=True) + jnp.sum(new, axis=1, keepdims=True)
        result = dot(old.astype(BF), old_values) + dot(new.astype(BF), fresh_values)
        result = result / total
        for head in range(8):
            for s in range(STEPS):
                start = head * 32 + s * 8
                att[
                    pl.ds(pl.multiple_of(s * SEQS + g * 8, 8), 8),
                    pl.ds(head * HEAD_DIM, HEAD_DIM),
                ] = result[start : start + 8]
        return carry

    lax.fori_loop(0, SEQS // 8, attend, 0)

    def settle(i, carry):
        rows = pl.ds(pl.multiple_of(i * 64, 64), 64)
        attb[rows, :] = att[rows, :].astype(BF)
        return carry

    lax.fori_loop(0, ROWS // 64, settle, 0)

    beside(send_o, arrive_o, 1, 1)
    beside(send_o, arrive_o, 1, 3)
    across(send_o, arrive_o, 0)
    across(send_o, arrive_o, 1)
    for dy in range(2):
        for dz in range(4):
            from_sibling(arrive_o, dy, dz)

    def partial(owner, rows):
        weights = obuf[pl.ds(owner * 2, 2)].reshape(Q_LOCAL, HALF)
        return dot(attb[rows, :], weights)

    sums = []
    for s, peer in enumerate(peers):
        def tiles(i, carry):
            rows = pl.ds(pl.multiple_of(i * 256, 256), 256)
            rs_send[s, rows, :] = partial(peer, rows).astype(BF)
            return carry

        lax.fori_loop(0, 2, tiles, 0)
        copy = pltpu.make_async_remote_copy(
            src_ref=rs_send.at[s],
            dst_ref=rs_recv.at[s],
            send_sem=rs_s.at[s],
            recv_sem=rs_r.at[s],
            device_id=at_tp(peer),
            device_id_type=MESH,
        )
        copy.start()
        sums.append(copy)

    def tiles_own(i, carry):
        rows = pl.ds(pl.multiple_of(i * 256, 256), 256)
        acc[0, rows, :] = partial(tp, rows)
        return carry

    lax.fori_loop(0, 2, tiles_own, 0)
    for copy in sums:
        copy.wait_recv()

    def finish(i, carry):
        rows = pl.ds(pl.multiple_of(i * 32, 32), 32)
        total = acc[0, rows, :]
        for s in range(7):
            total = total + rs_recv[s, rows, :].astype(F32)
        mixed[rows, :] = (resid[rows, :].astype(F32) + total * scales[3]).astype(BF)
        return carry

    lax.fori_loop(0, ROWS // 32, finish, 0)

    for copy in sums + sent_w + sent_o:
        copy.wait_send()


def shards(
    hidden_in,
    ln_gain,
    q_gain,
    k_gain,
    w_query,
    w_key,
    w_value,
    w_out,
    cache_keys,
    cache_values,
    cache_lengths,
    amax_history,
    cycle_pos,
):
    half_dim = HEAD_DIM // 2
    inverse = rope_base ** (-(2.0 * np.arange(half_dim)) / HEAD_DIM)
    freq = jnp.asarray(np.concatenate([inverse, inverse])[None, :], F32)
    vmem = pl.BlockSpec(memory_space=pltpu.VMEM)
    smem = pl.BlockSpec(memory_space=pltpu.SMEM)
    hbm = pl.BlockSpec(memory_space=pl.ANY)
    dma = pltpu.SemaphoreType.DMA
    mixed, new_history = pl.pallas_call(
        kernel,
        out_shape=(
            jax.ShapeDtypeStruct((ROWS, HALF), BF),
            jax.ShapeDtypeStruct((4, HIST), F32),
        ),
        in_specs=[hbm, vmem, vmem, vmem, vmem, vmem, vmem, vmem, hbm, hbm, vmem, vmem, smem]
        + [vmem] * 3,
        out_specs=(vmem, vmem),
        scratch_shapes=[
            pltpu.VMEM((SPOTS, ROWS, HALF), BF),
            pltpu.VMEM((SEQS, CACHE, HEAD_DIM), BF),
            pltpu.VMEM((SEQS, CACHE, HEAD_DIM), BF),
            pltpu.VMEM((TPS, PACKED, HALF), BF),
            pltpu.VMEM((REPS, TPS, PACKED, HALF), BF),
            pltpu.VMEM((REPS, 512, HALF), BF),
            pltpu.VMEM((1024, 384), BF),
            pltpu.VMEM((512, 384), BF),
            pltpu.VMEM((16, 128), BF),
            pltpu.VMEM((2, ROWS, HALF), F32),
            pltpu.VMEM((ROWS, Q_LOCAL), F32),
            pltpu.VMEM((ROWS, Q_LOCAL), BF),
            pltpu.VMEM((7, ROWS, HALF), BF),
            pltpu.VMEM((7, ROWS, HALF), BF),
            pltpu.VMEM((ROWS, HALF), BF),
            pltpu.VMEM((6, 8, 128), F32),
            pltpu.VMEM((12, 8, 128), F32),
            dma((12,)),
            dma((7,)),
            dma((7,)),
            dma((30,)),
            dma((REPS, 2)),
            dma((30,)),
            dma((REPS, 2)),
            dma(()),
            dma(()),
            dma((7,)),
            dma((7,)),
            dma((12,)),
            dma((12,)),
        ],
        compiler_params=pltpu.CompilerParams(
            collective_id=0, has_side_effects=True, vmem_limit_bytes=62 * 2**20
        ),
        cost_estimate=pl.CostEstimate(
            flops=13 * 10**9, bytes_accessed=13 * 10**6, transcendentals=10**6
        ),
    )(
        hidden_in.reshape(ROWS, D),
        ln_gain.reshape(1, D),
        q_gain.reshape(1, HEAD_DIM),
        k_gain.reshape(1, HEAD_DIM),
        w_query,
        w_key,
        w_value,
        w_out,
        cache_keys,
        cache_values,
        cache_lengths.reshape(SEQS, 1),
        amax_history,
        cycle_pos,
        jnp.asarray(spread_matrices(), BF),
        jnp.asarray(join_matrices(), BF),
        freq,
    )
    return mixed.reshape(STEPS, SEQS, HALF), new_history


def solution(mesh):
    placed = (
        P(None, "rep", None),
        P(),
        P(),
        P(),
        P(("rep", "tp"), None),
        P(("rep", "tp"), None),
        P(("rep", "tp"), None),
        P("tp", "rep"),
        P("rep", None, "tp"),
        P("rep", None, "tp"),
        P("rep"),
        P(),
        P(),
    )
    return jax.shard_map(
        shards, mesh=mesh, in_specs=placed, out_specs=(P(None, "rep", "tp"), P()), check_vma=False
    )
```

time: 733 us -> 221 us (0.30)
  the two profiles are of different devices: /device:TPU:1 before, /device:TPU:28 now
where the time goes in v1:
time: 221 us
  Pallas kernels  214 us (97%)
  local copies, waits for them, and re-layouts  6.86 us (3%)
    pallas_call x1, Pallas kernels, shards(): pl.pallas_call(kernel, out_shape=(jax.ShapeDtypeStruct((ROWS, HALF), BF),...  214 us
    unnamed x3, local copies, waits for them, and re-layouts  5.47 us

profile of v1, /device:TPU:28, one launch (start us, length us, event | category | flops | bytes accessed | tf_op | source)
XLA Modules:
  0.0 221.1 jit_solution(8199631214713940463)
XLA Ops:
  0.6 1.4 copy.19.lengths
  2.0 2.2 %copy.18.w_out = bf16[1024,320]{1,0:T(8,128)(2,1)} copy(bf16[1024,320]{0,1:T(8,128)(2,1)} %param.23) | data formatting | bytes 1310720 | tf_op args[7]
  4.3 213.6 %shard_map.167 = (bf16[512,640]{1,0:T(8,128)(2,1)}, f32[4,16]{1,0:T(4,128)}) custom-call(bf16[512,5120]{1,0:T(8,128)(2,1)} %bitcast.8, f32[1,5120]{1,0:T(1,128)} %bitcast.9, f32[1,128]{1,0:T(1,128)} %bitcast.10, f32[1,128]{1,0:T(1,128)} %bitcast.11, bf16[40,8192]{1,0:T(8,128)(2,1)} %w_query.1, bf16[40,1024]{1,0:T(8,128)(2,1)} %w_key.1, ...), custom_call_target="tpu_custom_call" | custom-call | flops 12999999488 | bytes 13000000 | tf_op jit(solution)/shard_map/pallas_call | solution.py:588
  217.8 2.0 copy.22
  219.8 1.2 copy.23

commit v2 on v1

v2 whole, which is shorter than its diff:
```python
import jax
import jax.numpy as jnp
import numpy as np
from jax import lax
from jax.experimental import pallas as pl
from jax.experimental.pallas import tpu as pltpu
from jax.sharding import PartitionSpec as P

D = 5120
HEADS = 64
KV_HEADS = 8
HEAD_DIM = 128
STEPS = 4
HIST = 16
WINDOW = 8
Q_WIDTH = 8192
CACHE = 64
SEQS = 128
ROWS = STEPS * SEQS
REPS = 16
TPS = 8
SPOTS = 8
SHARD = 40
Q_LOCAL = 1024
HALF = 640
PACKED = 80
OUT_SHARD = 320
W_PIECES = ((0, 3), (3, 2), (5, 1), (6, 2))
O_PIECES = ((0, 160), (160, 160))

fp8_top = 448.0
rope_base = 1000000.0
norm_eps = 1e-06

BF = jnp.bfloat16
F32 = jnp.float32
MESH = pl.DeviceIdType.MESH


def dot(a, b):
    return jnp.dot(a, b, preferred_element_type=F32)


def quantize(weight, factor):
    return jnp.clip(weight.astype(F32) / factor, -fp8_top, fp8_top)


def kernel(
    hidden,
    ln_gain,
    q_gain,
    k_gain,
    w_query,
    w_key,
    w_value,
    w_out,
    cache_keys,
    cache_values,
    lengths,
    history,
    cycle,
    freq,
    mixed,
    new_history,
    rows_in,
    keys_in,
    values_in,
    stage,
    wbuf,
    obuf,
    spread,
    xs,
    tables,
    seq_len,
    acc,
    own_hi,
    attb,
    rs_recv,
    resid,
    amax_out,
    amax_in,
    local_sem,
    a2a_s,
    a2a_r,
    w_s,
    w_r,
    o_s,
    o_r,
    rs_s,
    rs_r,
    am_s,
    am_r,
):
    rep = lax.axis_index("rep")
    tp = lax.axis_index("tp")
    yh = rep // 8
    zz = (rep // 2) % 4
    core = rep % 2
    spot = rep // 2

    def rep_of(dy, dz, flip):
        return ((yh + dy) % 2) * 8 + ((zz + dz) % 4) * 2 + (core + flip) % 2

    def spot_of(dy, dz):
        return ((yh + dy) % 2) * 4 + (zz + dz) % 4

    def at_rep(index):
        return {"rep": index, "tp": tp}

    def at_tp(index):
        return {"rep": rep, "tp": index}

    peers = [(tp + s) % TPS for s in range(1, TPS)]
    y_far = rep_of(1, 0, 0)
    z_up = rep_of(0, 1, 0)
    z_down = rep_of(0, 3, 0)
    sibling = rep_of(0, 0, 1)
    line_x = tp // 2
    line_y = tp % 2

    loads = []
    for i in range(SPOTS):
        loads.append(
            pltpu.make_async_copy(hidden.at[:, pl.ds(i * HALF, HALF)], rows_in.at[i], local_sem.at[i])
        )
    loads.append(pltpu.make_async_copy(cache_keys, keys_in, local_sem.at[8]))
    loads.append(pltpu.make_async_copy(cache_values, values_in, local_sem.at[9]))
    loads.append(
        pltpu.make_async_copy(
            hidden.at[:, pl.ds(pl.multiple_of(tp * HALF, 128), HALF)], resid, local_sem.at[10]
        )
    )
    for load in loads:
        load.start()

    barrier = pltpu.get_barrier_semaphore()
    for peer in peers:
        pl.semaphore_signal(barrier, inc=1, device_id=at_tp(peer), device_id_type=MESH)
    for other in (y_far, z_up, z_down, sibling):
        pl.semaphore_signal(barrier, inc=1, device_id=at_rep(other), device_id_type=MESH)

    slot = lax.broadcasted_iota(jnp.int32, (1, HIST), 1)
    fans = (D, D, D, Q_WIDTH)
    roots = [float(np.sqrt(np.float32(fan))) for fan in fans]
    scales = []
    for m in range(4):
        behind = jnp.bitwise_and(cycle[m] + (2 * HIST - 1) - slot, HIST - 1)
        limit = jnp.max(
            jnp.where(behind < WINDOW, history[m : m + 1, :], 0.0), axis=1, keepdims=True
        )
        scales.append(limit / (fp8_top * roots[m]))

    def pack(j, tops):
        query = w_query[:, pl.ds(pl.multiple_of(j * Q_LOCAL, 128), Q_LOCAL)]
        key = w_key[:, pl.ds(pl.multiple_of(j * 128, 128), 128)]
        value = w_value[:, pl.ds(pl.multiple_of(j * 128, 128), 128)]
        q0 = quantize(query, scales[0])
        k0 = quantize(key, scales[1])
        v0 = quantize(value, scales[2])
        first = q0[:, :HALF]
        second = jnp.concatenate([q0[:, HALF:], k0, v0], axis=1)
        stage[j, 0:32, :] = first[0:32].astype(BF)
        stage[j, 32:48, :] = jnp.concatenate([first[32:40], second[32:40]], axis=0).astype(BF)
        stage[j, 48:80, :] = second[0:32].astype(BF)

        def top(values, old):
            found = jnp.max(jnp.abs(values.astype(F32)), axis=0, keepdims=True)
            for i in range(values.shape[1] // 128):
                old = jnp.maximum(old, found[:, i * 128 : (i + 1) * 128])
            return old

        return top(query, tops[0]), top(key, tops[1]), top(value, tops[2])

    none = jnp.zeros((1, 128), F32)
    tops = lax.fori_loop(0, TPS, pack, (none, none, none))

    pl.semaphore_wait(barrier, 11)

    a2a = []
    for s, peer in enumerate(peers):
        a2a.append(
            pltpu.make_async_remote_copy(
                src_ref=stage.at[peer],
                dst_ref=wbuf.at[rep, tp],
                send_sem=a2a_s.at[s],
                recv_sem=a2a_r.at[s],
                device_id=at_tp(peer),
                device_id_type=MESH,
            )
        )
    for copy in a2a:
        copy.start()
    own_plane = pltpu.make_async_copy(stage.at[tp], wbuf.at[rep, tp], local_sem.at[11])
    own_plane.start()

    def pack_out(i, old):
        rows = pl.ds(pl.multiple_of(i * 32, 32), 32)
        shard = w_out[rows, :]
        obuf[rep, rows, :] = quantize(shard, scales[3]).astype(BF)
        found = jnp.max(jnp.abs(shard.astype(F32)), axis=0, keepdims=True)
        return jnp.maximum(old, jnp.max(found, axis=1, keepdims=True))

    top_out = lax.fori_loop(0, OUT_SHARD // 32, pack_out, jnp.zeros((1, 1), F32))

    tile_row = lax.broadcasted_iota(jnp.int32, (8, 128), 0)
    found = [jnp.max(top, axis=1, keepdims=True) for top in tops] + [top_out]
    tile = jnp.zeros((8, 128), F32)
    for m in range(4):
        tile = jnp.where(tile_row == m, found[m], tile)
    amax_out[0] = tile

    def send_amax(stage_index, slot_index, where):
        return pltpu.make_async_remote_copy(
            src_ref=amax_out.at[stage_index],
            dst_ref=amax_in.at[slot_index],
            send_sem=am_s.at[slot_index],
            recv_sem=am_r.at[slot_index],
            device_id=where,
            device_id_type=MESH,
        )

    am_tp = [send_amax(0, s, at_tp(peer)) for s, peer in enumerate(peers)]
    am_y = [send_amax(1, 7, at_rep(y_far))]
    am_z = [send_amax(2, 8, at_rep(z_up)), send_amax(2, 9, at_rep(z_down))]
    am_w = [send_amax(3, 10, at_rep(z_up))]
    am_c = [send_amax(4, 11, at_rep(sibling))]

    def fold(copies, index, slots):
        for copy in copies:
            copy.wait()
        total = amax_out[index]
        for where in slots:
            total = jnp.maximum(total, amax_in[where])
        amax_out[index + 1] = total

    for copy in am_tp:
        copy.start()

    for load in loads[:8]:
        load.wait()

    def norm(i, carry):
        rows = pl.ds(pl.multiple_of(i * 32, 32), 32)
        parts = [rows_in[j, rows, :].astype(F32) for j in range(SPOTS)]
        square = parts[0] * parts[0]
        for part in parts[1:]:
            square = square + part * part
        mean = jnp.sum(square, axis=1, keepdims=True) / D
        factor = lax.rsqrt(mean + norm_eps)
        for j in range(SPOTS):
            gain = ln_gain[0:1, j * HALF : (j + 1) * HALF]
            rows_in[j, rows, :] = (parts[j] * factor * gain).astype(BF)
        return carry

    lax.fori_loop(0, ROWS // 32, norm, 0)

    def relay(buf, pieces, send_sem, recv_sem):
        sent = []

        def send(block, piece, *targets):
            view = buf.at[block, pl.ds(*pieces[piece])]
            for target in targets:
                copy = pltpu.make_async_remote_copy(
                    src_ref=view,
                    dst_ref=view,
                    send_sem=send_sem.at[len(sent)],
                    recv_sem=recv_sem.at[block, piece],
                    device_id=at_rep(target),
                    device_id_type=MESH,
                )
                copy.start()
                sent.append(copy)

        def arrive(block, *which):
            for piece in which or range(len(pieces)):
                view = buf.at[block, pl.ds(*pieces[piece])]
                pltpu.make_async_remote_copy(
                    src_ref=view,
                    dst_ref=view,
                    send_sem=send_sem.at[0],
                    recv_sem=recv_sem.at[block, piece],
                    device_id=at_rep(sibling),
                    device_id_type=MESH,
                ).wait_recv()

        return send, arrive, sent

    send_w, arrive_w, sent_w = relay(wbuf, W_PIECES, w_s, w_r)
    send_o, arrive_o, sent_o = relay(obuf, O_PIECES, o_s, o_r)

    def both_w(dy, dz):
        arrive_w(rep_of(dy, dz, 1))

    def both_o(dy, dz):
        arrive_o(rep_of(dy, dz, 1))

    def far_o():
        for piece in range(2):
            arrive_o(y_far, piece)
            send_o(y_far, piece, z_up, z_down, sibling)

    def beside_o(dy):
        for piece in range(2):
            for dz, target, keep in ((1, z_down, 0), (3, z_up, 1)):
                block = rep_of(dy, dz, 0)
                arrive_o(block, piece)
                if piece == keep:
                    send_o(block, piece, target)
                send_o(block, piece, sibling)

    def across_o(dy):
        for piece in range(2):
            arrive_o(rep_of(dy, 2, 0), piece)
            send_o(rep_of(dy, 2, 0), piece, sibling)

    for piece in range(2):
        send_o(rep, piece, z_up, z_down, y_far, sibling)

    diagonal = lax.broadcasted_iota(jnp.int32, (SEQS, SEQS), 0) == lax.broadcasted_iota(
        jnp.int32, (SEQS, SEQS), 1
    )
    seq_len[...] = jnp.sum(
        jnp.where(diagonal, lengths[...].astype(F32), 0.0), axis=1, keepdims=True
    )
    lane = lax.broadcasted_iota(jnp.int32, (SEQS, HEAD_DIM), 1)

    def turn(s, carry):
        rows = pl.ds(pl.multiple_of(s * SEQS, SEQS), SEQS)
        angles = (seq_len[...] + lax.convert_element_type(s, F32)) * freq[...]
        tables[0, rows, :] = jnp.cos(angles)
        sine = jnp.sin(angles)
        tables[1, rows, :] = jnp.where(lane < 64, -sine, sine)
        return carry

    column = lax.broadcasted_iota(jnp.int32, (1, 768), 1)
    block_of = jnp.right_shift(column * 1366, 16)
    inside = column - block_of * 48
    wanted = (
        jnp.where(inside < 40, block_of * SHARD + inside, -1),
        jnp.where(
            inside < 8,
            -1,
            block_of * SHARD + jnp.where(inside < 16, inside + 24, inside - 16),
        ),
    )
    for h in range(2):
        for part in range(5):
            row = lax.broadcasted_iota(jnp.int32, (128, 768), 0) + part * 128
            spread[h, part * 128 : (part + 1) * 128, :] = jnp.where(
                row == wanted[h], 1.0, 0.0
            ).astype(BF)

    lax.fori_loop(0, STEPS, turn, 0)
    own_plane.wait()
    for copy in a2a:
        copy.wait()

    send_w(rep, 0, y_far)
    send_w(rep, 1, y_far)
    send_w(rep, 2, z_up, z_down, sibling)
    send_w(rep, 3, z_up, z_down, sibling)
    send_w(rep, 0, z_up, z_down, sibling)
    send_w(rep, 1, z_up, z_down, sibling)
    send_w(rep, 2, y_far)
    send_w(rep, 3, y_far)

    acc[...] = jnp.zeros_like(acc)

    def select(dy, dz):
        place = spot_of(dy, dz)

        def tiles(i, carry):
            rows = pl.ds(pl.multiple_of(i * 256, 256), 256)
            for h in range(2):
                xs[place, h, rows, :] = dot(rows_in[place, rows, :], spread[h]).astype(BF)
            return carry

        lax.fori_loop(0, 2, tiles, 0)

    def project(dy, dz):
        place = spot_of(dy, dz)

        def tiles(i, carry):
            rows = pl.ds(pl.multiple_of(i * 256, 256), 256)
            for h in range(2):
                block = wbuf[pl.ds(place * 2, 2), :, h * 32 : h * 32 + 48, :].reshape(768, HALF)
                acc[h, rows, :] = acc[h, rows, :] + dot(xs[place, h, rows, :], block)
            return carry

        lax.fori_loop(0, 2, tiles, 0)

    select(0, 0)
    select(1, 0)
    for piece in (2, 3):
        for dz, target, keep in ((1, z_down, 2), (3, z_up, 3)):
            block = rep_of(0, dz, 0)
            arrive_w(block, piece)
            if piece == keep:
                send_w(block, piece, target)
            send_w(block, piece, y_far, sibling)
    select(0, 1)
    for piece in (0, 1):
        arrive_w(y_far, piece)
        send_w(y_far, piece, z_up, z_down, sibling)
    both_w(0, 0)
    project(0, 0)
    select(0, 3)
    fold(am_tp, 0, range(7))
    am_y[0].start()
    for piece in (0, 1):
        for dz, target, keep in ((1, z_down, 0), (3, z_up, 1)):
            block = rep_of(0, dz, 0)
            arrive_w(block, piece)
            if piece == keep:
                send_w(block, piece, target)
            send_w(block, piece, sibling)
    for piece in (2, 3):
        arrive_w(y_far, piece)
        send_w(y_far, piece, sibling)
    both_w(0, 1)
    project(0, 1)
    select(1, 1)
    for piece in (2, 3):
        arrive_w(rep_of(0, 2, 0), piece)
        send_w(rep_of(0, 2, 0), piece, y_far, sibling)
    both_w(0, 3)
    project(0, 3)
    both_w(1, 0)
    project(1, 0)
    select(1, 3)
    fold(am_y, 1, [7])
    for copy in am_z:
        copy.start()
    for piece in (2, 3):
        for dz in (1, 3):
            arrive_w(rep_of(1, dz, 0), piece)
            send_w(rep_of(1, dz, 0), piece, sibling)
    select(0, 2)
    for piece in (0, 1):
        for dz, target, keep in ((1, z_down, 0), (3, z_up, 1)):
            block = rep_of(1, dz, 0)
            arrive_w(block, piece)
            if piece == keep:
                send_w(block, piece, target)
            send_w(block, piece, sibling)
    select(1, 2)
    both_w(1, 1)
    project(1, 1)
    fold(am_z, 2, [8, 9])
    am_w[0].start()
    for piece in (0, 1):
        arrive_w(rep_of(0, 2, 0), piece)
        send_w(rep_of(0, 2, 0), piece, sibling)
    far_o()
    beside_o(0)
    both_w(1, 3)
    project(1, 3)
    both_w(0, 2)
    project(0, 2)
    fold(am_w, 3, [10])
    am_c[0].start()
    for piece in (2, 3, 0, 1):
        arrive_w(rep_of(1, 2, 0), piece)
        send_w(rep_of(1, 2, 0), piece, sibling)
    both_w(1, 2)
    project(1, 2)

    def head_norm(s, carry):
        rows = pl.ds(pl.multiple_of(s * SEQS, SEQS), SEQS)
        cosine = tables[0, rows, :]
        sine = tables[1, rows, :]
        for head in range(9):
            h, lanes = (0, head) if head < 5 else (1, head - 5)
            cols = pl.ds(lanes * HEAD_DIM, HEAD_DIM)
            values = acc[h, rows, cols]
            gain = q_gain[...] if head < 8 else k_gain[...]
            mean = jnp.sum(values * values, axis=1, keepdims=True) / HEAD_DIM
            values = values * lax.rsqrt(mean + norm_eps) * gain
            acc[h, rows, cols] = values * cosine + pltpu.roll(values, 64, 1) * sine
        cols = pl.ds(512, HEAD_DIM)
        acc[1, rows, cols] = acc[1, rows, cols] * scales[2]
        return carry

    lax.fori_loop(0, STEPS, head_norm, 0)

    for load in loads[8:]:
        load.wait()

    old_seq = lax.broadcasted_iota(jnp.int32, (8, 8 * CACHE), 0)
    old_col = lax.broadcasted_iota(jnp.int32, (8, 8 * CACHE), 1)
    old_slot = jnp.where(
        jnp.right_shift(old_col, 6) == old_seq, jnp.bitwise_and(old_col, CACHE - 1), CACHE
    ).astype(F32)
    new_row = lax.broadcasted_iota(jnp.int32, (32, 32), 0)
    new_col = lax.broadcasted_iota(jnp.int32, (32, 32), 1)
    new_live = (jnp.bitwise_and(new_row, 7) == jnp.bitwise_and(new_col, 7)) & (
        jnp.right_shift(new_col, 3) <= jnp.right_shift(new_row, 3)
    )
    new_bias = jnp.where(new_live, 0.0, -1e30)
    scaling = HEAD_DIM ** (-0.5)
    nt = (((1,), (1,)), ((), ()))

    def attend_eight(g):
        seqs = pl.ds(pl.multiple_of(g * 8, 8), 8)

        def pick(h, lanes):
            return [
                acc[h, pl.ds(pl.multiple_of(s * SEQS + g * 8, 8), 8), pl.ds(lanes * HEAD_DIM, HEAD_DIM)]
                for s in range(STEPS)
            ]

        rows = []
        for head in range(8):
            rows += pick(0, head) if head < 5 else pick(1, head - 5)
        queries = jnp.concatenate(rows, axis=0).astype(BF)
        fresh_keys = jnp.concatenate(pick(1, 3), axis=0).astype(BF)
        fresh_values = jnp.concatenate(pick(1, 4), axis=0).astype(BF)
        old_keys = keys_in[seqs].reshape(8 * CACHE, HEAD_DIM)
        old_values = values_in[seqs].reshape(8 * CACHE, HEAD_DIM)
        old_bias = jnp.where(old_slot < seq_len[seqs, :], 0.0, -1e30)
        old = lax.dot_general(queries, old_keys, nt, preferred_element_type=F32)
        new = lax.dot_general(queries, fresh_keys, nt, preferred_element_type=F32)
        old = (old.reshape(32, 8, 8 * CACHE) * scaling + old_bias[None]).reshape(256, 8 * CACHE)
        new = (new.reshape(8, 32, 32) * scaling + new_bias[None]).reshape(256, 32)
        top = jnp.maximum(
            jnp.max(old, axis=1, keepdims=True), jnp.max(new, axis=1, keepdims=True)
        )
        old = jnp.exp(old - top)
        new = jnp.exp(new - top)
        total = jnp.sum(old, axis=1, keepdims=True) + jnp.sum(new, axis=1, keepdims=True)
        result = dot(old.astype(BF), old_values) + dot(new.astype(BF), fresh_values)
        return result / total

    def attend(g, carry):
        low = attend_eight(g * 2)
        high = attend_eight(g * 2 + 1)
        for head in range(8):
            for s in range(STEPS):
                start = head * 32 + s * 8
                pair = jnp.concatenate([low[start : start + 8], high[start : start + 8]], axis=0)
                attb[
                    pl.ds(pl.multiple_of(s * SEQS + g * 16, 16), 16),
                    pl.ds(head * HEAD_DIM, HEAD_DIM),
                ] = pair.astype(BF)
        return carry

    lax.fori_loop(0, SEQS // 16, attend, 0)

    beside_o(1)
    for dy in range(2):
        for dz in (1, 3):
            both_o(dy, dz)

    lo = pl.ds(0, 256)
    hi = pl.ds(256, 256)

    def slot_of(index):
        return rows_in.at[index // 2, pl.ds((index % 2) * 256, 256)]

    def push(index, target):
        return pltpu.make_async_remote_copy(
            src_ref=slot_of(index),
            dst_ref=rs_recv.at[index],
            send_sem=rs_s.at[index],
            recv_sem=rs_r.at[index],
            device_id=at_tp(target),
            device_id_type=MESH,
        )

    def put(index, values):
        rows_in[index // 2, pl.ds((index % 2) * 256, 256), :] = values.astype(BF)

    across_x = [((line_x + k) % 4) * 2 + line_y for k in range(4)]
    y_mate = line_x * 2 + 1 - line_y
    to_mate = [push(k, y_mate) for k in range(4)]
    other_x = [push(3 + k, across_x[k]) for k in range(1, 4)]
    this_hi = [push(6 + k, across_x[k]) for k in range(1, 4)]
    this_lo = [push(9 + k, across_x[k]) for k in range(1, 4)]
    last = push(13, y_mate)

    def partial(k, row, rows):
        owner = ((line_x + k) % 4) * 2 + row
        weights = obuf[pl.ds(owner * 2, 2)].reshape(HALF, Q_LOCAL)
        return lax.dot_general(attb[rows, :], weights, nt, preferred_element_type=F32)

    def other_row():
        for k in (1, 2, 3, 0):
            put(k, partial(k, 1 - line_y, lo))
            to_mate[k].start()
            values = partial(k, 1 - line_y, hi)
            if k:
                put(3 + k, values)
                other_x[k - 1].start()
            else:
                own_hi[0] = values

    def this_row():
        for k in (1, 2, 3, 0):
            values = partial(k, line_y, hi)
            if k:
                put(6 + k, values)
                this_hi[k - 1].start()
            else:
                own_hi[1] = values
            acc[k // 2, pl.ds((k % 2) * 256, 256), :] = partial(k, line_y, lo)

    other_first = (zz + 1) % 2 == 1 - line_y
    pl.when(other_first)(other_row)
    pl.when(jnp.logical_not(other_first))(this_row)
    across_o(0)
    across_o(1)
    for dy in range(2):
        for dz in (0, 2):
            both_o(dy, dz)
    pl.when(other_first)(this_row)
    pl.when(jnp.logical_not(other_first))(other_row)

    for k in (1, 2, 3):
        to_mate[k].wait_recv()
        put(9 + k, acc[k // 2, pl.ds((k % 2) * 256, 256), :] + rs_recv[k].astype(F32))
        this_lo[k - 1].start()
    for copy in other_x:
        copy.wait_recv()
    total = own_hi[0]
    for k in (1, 2, 3):
        total = total + rs_recv[3 + k].astype(F32)
    put(13, total)
    last.start()
    to_mate[0].wait_recv()

    def finish(first, gathered, base):
        def step(i, carry):
            rows = pl.ds(pl.multiple_of(i * 32, 32), 32)
            outs = pl.ds(pl.multiple_of(first + i * 32, 32), 32)
            total = base[rows, :]
            for index in gathered:
                total = total + rs_recv[index, rows, :].astype(F32)
            mixed[outs, :] = (resid[outs, :].astype(F32) + total * scales[3]).astype(BF)
            return carry

        lax.fori_loop(0, 8, step, 0)

    for copy in this_lo:
        copy.wait_recv()
    finish(0, (0, 10, 11, 12), acc.at[0])
    for copy in this_hi:
        copy.wait_recv()
    last.wait_recv()
    finish(256, (7, 8, 9, 13), own_hi.at[1])

    for copy in to_mate + other_x + this_hi + this_lo + [last] + sent_w + sent_o:
        copy.wait_send()
    fold(am_c, 4, [11])
    for m in range(4):
        new_history[m : m + 1, :] = jnp.where(
            slot == cycle[m],
            amax_out[5, m : m + 1, 0:1] * roots[m],
            history[m : m + 1, :],
        )


def shards(
    hidden_in,
    ln_gain,
    q_gain,
    k_gain,
    w_query,
    w_key,
    w_value,
    w_out,
    cache_keys,
    cache_values,
    cache_lengths,
    amax_history,
    cycle_pos,
):
    half_dim = HEAD_DIM // 2
    inverse = rope_base ** (-(2.0 * np.arange(half_dim)) / HEAD_DIM)
    freq = jnp.asarray(np.concatenate([inverse, inverse])[None, :], F32)
    vmem = pl.BlockSpec(memory_space=pltpu.VMEM)
    smem = pl.BlockSpec(memory_space=pltpu.SMEM)
    hbm = pl.BlockSpec(memory_space=pl.ANY)
    dma = pltpu.SemaphoreType.DMA
    mixed, new_history = pl.pallas_call(
        kernel,
        out_shape=(
            jax.ShapeDtypeStruct((ROWS, HALF), BF),
            jax.ShapeDtypeStruct((4, HIST), F32),
        ),
        in_specs=[hbm, vmem, vmem, vmem, vmem, vmem, vmem, vmem, hbm, hbm, vmem, vmem, smem]
        + [vmem],
        out_specs=(vmem, vmem),
        scratch_shapes=[
            pltpu.VMEM((SPOTS, ROWS, HALF), BF),
            pltpu.VMEM((SEQS, CACHE, HEAD_DIM), BF),
            pltpu.VMEM((SEQS, CACHE, HEAD_DIM), BF),
            pltpu.VMEM((TPS, PACKED, HALF), BF),
            pltpu.VMEM((REPS, TPS, PACKED, HALF), BF),
            pltpu.VMEM((REPS, OUT_SHARD, Q_LOCAL), BF),
            pltpu.VMEM((2, HALF, 768), BF),
            pltpu.VMEM((SPOTS, 2, ROWS, 768), BF),
            pltpu.VMEM((2, ROWS, HEAD_DIM), F32),
            pltpu.VMEM((SEQS, 1), F32),
            pltpu.VMEM((2, ROWS, HALF), F32),
            pltpu.VMEM((2, 256, HALF), F32),
            pltpu.VMEM((ROWS, Q_LOCAL), BF),
            pltpu.VMEM((14, 256, HALF), BF),
            pltpu.VMEM((ROWS, HALF), BF),
            pltpu.VMEM((6, 8, 128), F32),
            pltpu.VMEM((12, 8, 128), F32),
            dma((12,)),
            dma((7,)),
            dma((7,)),
            dma((60,)),
            dma((REPS, 4)),
            dma((30,)),
            dma((REPS, 2)),
            dma((14,)),
            dma((14,)),
            dma((12,)),
            dma((12,)),
        ],
        compiler_params=pltpu.CompilerParams(
            collective_id=0, has_side_effects=True, vmem_limit_bytes=62 * 2**20
        ),
        cost_estimate=pl.CostEstimate(
            flops=13 * 10**9, bytes_accessed=13 * 10**6, transcendentals=10**6
        ),
    )(
        hidden_in.reshape(ROWS, D),
        ln_gain.reshape(1, D),
        q_gain.reshape(1, HEAD_DIM),
        k_gain.reshape(1, HEAD_DIM),
        w_query,
        w_key,
        w_value,
        w_out.T,
        cache_keys,
        cache_values,
        cache_lengths.reshape(1, SEQS),
        amax_history,
        cycle_pos,
        freq,
    )
    return mixed.reshape(STEPS, SEQS, HALF), new_history


def solution(mesh):
    placed = (
        P(None, "rep", None),
        P(),
        P(),
        P(),
        P(("rep", "tp"), None),
        P(("rep", "tp"), None),
        P(("rep", "tp"), None),
        P("tp", "rep"),
        P("rep", None, "tp"),
        P("rep", None, "tp"),
        P("rep"),
        P(),
        P(),
    )
    return jax.shard_map(
        shards, mesh=mesh, in_specs=placed, out_specs=(P(None, "rep", "tp"), P()), check_vma=False
    )
```

time: 221 us -> 149 us (0.67)
  the two profiles are of different devices: /device:TPU:28 before, /device:TPU:1 now
where the time goes in v2:
time: 149 us
  Pallas kernels  145 us (97%)
  local copies, waits for them, and re-layouts  3.23 us (2%)
    pallas_call x1, Pallas kernels, shards(): pl.pallas_call(kernel, out_shape=(jax.ShapeDtypeStruct((ROWS, HALF), BF),...  145 us
    unnamed x2, local copies, waits for them, and re-layouts  3.23 us

profile of v2, /device:TPU:1, one launch (start us, length us, event | category | flops | bytes accessed | tf_op | source)
XLA Modules:
  0.0 148.9 jit_solution(3017949001402064782)
XLA Ops:
  0.6 145.0 %shard_map.149 = (bf16[512,640]{1,0:T(8,128)(2,1)}, f32[4,16]{1,0:T(4,128)}) custom-call(bf16[512,5120]{1,0:T(8,128)(2,1)} %bitcast.8, f32[1,5120]{1,0:T(1,128)} %bitcast.10, f32[1,128]{1,0:T(1,128)} %bitcast.11, f32[1,128]{1,0:T(1,128)} %bitcast.12, bf16[40,8192]{1,0:T(8,128)(2,1)} %w_query.1, bf16[40,1024]{1,0:T(8,128)(2,1)} %w_key.1, ...), custom_call_target="tpu_custom_call" | custom-call | flops 12999999488 | bytes 13000000 | tf_op jit(solution)/shard_map/pallas_call | solution.py:684
  145.6 2.0 %copy.18 = bf16[4,128,640]{2,1,0:T(8,128)(2,1)} copy(bf16[4,128,640]{2,1,0:T(8,128)(2,1)} %bitcast.7) | data formatting | bytes 1310720
  147.6 1.2 copy.19

commit v3 on v2

--- a/solution.py
+++ b/solution.py
@@ -25,7 +25,9 @@
 HALF = 640
 PACKED = 80
 OUT_SHARD = 320
-W_PIECES = ((0, 3), (3, 2), (5, 1), (6, 2))
+LOW = 224
+PLANES = ((0, 0), (0, 1), (1, 0), (3, 0), (1, 1), (3, 1), (2, 0), (2, 1))
+W_PIECES = ((5, 3), (2, 3), (0, 1), (1, 1))
 O_PIECES = ((0, 160), (160, 160))
 
 fp8_top = 448.0
@@ -73,7 +75,6 @@
     tables,
     seq_len,
     acc,
-    own_hi,
     attb,
     rs_recv,
     resid,
@@ -110,13 +111,13 @@
     def at_tp(index):
         return {"rep": rep, "tp": index}
 
-    peers = [(tp + s) % TPS for s in range(1, TPS)]
     y_far = rep_of(1, 0, 0)
     z_up = rep_of(0, 1, 0)
     z_down = rep_of(0, 3, 0)
     sibling = rep_of(0, 0, 1)
     line_x = tp // 2
     line_y = tp % 2
+    peers = [((line_x + kx) % 4) * 2 + (line_y + ky) % 2 for kx, ky in PLANES[1:]]
 
     loads = []
     for i in range(SPOTS):
@@ -181,7 +182,7 @@
         a2a.append(
             pltpu.make_async_remote_copy(
                 src_ref=stage.at[peer],
-                dst_ref=wbuf.at[rep, tp],
+                dst_ref=wbuf.at[rep, s + 1],
                 send_sem=a2a_s.at[s],
                 recv_sem=a2a_r.at[s],
                 device_id=at_tp(peer),
@@ -190,69 +191,8 @@
         )
     for copy in a2a:
         copy.start()
-    own_plane = pltpu.make_async_copy(stage.at[tp], wbuf.at[rep, tp], local_sem.at[11])
+    own_plane = pltpu.make_async_copy(stage.at[tp], wbuf.at[rep, 0], local_sem.at[11])
     own_plane.start()
-
-    def pack_out(i, old):
-        rows = pl.ds(pl.multiple_of(i * 32, 32), 32)
-        shard = w_out[rows, :]
-        obuf[rep, rows, :] = quantize(shard, scales[3]).astype(BF)
-        found = jnp.max(jnp.abs(shard.astype(F32)), axis=0, keepdims=True)
-        return jnp.maximum(old, jnp.max(found, axis=1, keepdims=True))
-
-    top_out = lax.fori_loop(0, OUT_SHARD // 32, pack_out, jnp.zeros((1, 1), F32))
-
-    tile_row = lax.broadcasted_iota(jnp.int32, (8, 128), 0)
-    found = [jnp.max(top, axis=1, keepdims=True) for top in tops] + [top_out]
-    tile = jnp.zeros((8, 128), F32)
-    for m in range(4):
-        tile = jnp.where(tile_row == m, found[m], tile)
-    amax_out[0] = tile
-
-    def send_amax(stage_index, slot_index, where):
-        return pltpu.make_async_remote_copy(
-            src_ref=amax_out.at[stage_index],
-            dst_ref=amax_in.at[slot_index],
-            send_sem=am_s.at[slot_index],
-            recv_sem=am_r.at[slot_index],
-            device_id=where,
-            device_id_type=MESH,
-        )
-
-    am_tp = [send_amax(0, s, at_tp(peer)) for s, peer in enumerate(peers)]
-    am_y = [send_amax(1, 7, at_rep(y_far))]
-    am_z = [send_amax(2, 8, at_rep(z_up)), send_amax(2, 9, at_rep(z_down))]
-    am_w = [send_amax(3, 10, at_rep(z_up))]
-    am_c = [send_amax(4, 11, at_rep(sibling))]
-
-    def fold(copies, index, slots):
-        for copy in copies:
-            copy.wait()
-        total = amax_out[index]
-        for where in slots:
-            total = jnp.maximum(total, amax_in[where])
-        amax_out[index + 1] = total
-
-    for copy in am_tp:
-        copy.start()
-
-    for load in loads[:8]:
-        load.wait()
-
-    def norm(i, carry):
-        rows = pl.ds(pl.multiple_of(i * 32, 32), 32)
-        parts = [rows_in[j, rows, :].astype(F32) for j in range(SPOTS)]
-        square = parts[0] * parts[0]
-        for part in parts[1:]:
-            square = square + part * part
-        mean = jnp.sum(square, axis=1, keepdims=True) / D
-        factor = lax.rsqrt(mean + norm_eps)
-        for j in range(SPOTS):
-            gain = ln_gain[0:1, j * HALF : (j + 1) * HALF]
-            rows_in[j, rows, :] = (parts[j] * factor * gain).astype(BF)
-        return carry
-
-    lax.fori_loop(0, ROWS // 32, norm, 0)
 
     def relay(buf, pieces, send_sem, recv_sem):
         sent = []
@@ -313,8 +253,92 @@
             arrive_o(rep_of(dy, 2, 0), piece)
             send_o(rep_of(dy, 2, 0), piece, sibling)
 
+    own_plane.wait()
+    send_w(rep, 2, z_up, z_down, y_far, sibling)
+
+    def pack_out(i, old):
+        rows = pl.ds(pl.multiple_of(i * 32, 32), 32)
+        shard = w_out[rows, :]
+        obuf[rep, rows, :] = quantize(shard, scales[3]).astype(BF)
+        found = jnp.max(jnp.abs(shard.astype(F32)), axis=0, keepdims=True)
+        return jnp.maximum(old, jnp.max(found, axis=1, keepdims=True))
+
+    top_out = lax.fori_loop(0, OUT_SHARD // 32, pack_out, jnp.zeros((1, 1), F32))
+
+    a2a[0].wait_recv()
+    send_w(rep, 3, z_up, z_down, y_far, sibling)
     for piece in range(2):
-        send_o(rep, piece, z_up, z_down, y_far, sibling)
+        send_o(rep, piece, z_up, z_down, sibling)
+
+    tile_row = lax.broadcasted_iota(jnp.int32, (8, 128), 0)
+    found = [jnp.max(top, axis=1, keepdims=True) for top in tops] + [top_out]
+    tile = jnp.zeros((8, 128), F32)
+    for m in range(4):
+        tile = jnp.where(tile_row == m, found[m], tile)
+    amax_out[0] = tile
+
+    def send_amax(stage_index, slot_index, where):
+        return pltpu.make_async_remote_copy(
+            src_ref=amax_out.at[stage_index],
+            dst_ref=amax_in.at[slot_index],
+            send_sem=am_s.at[slot_index],
+            recv_sem=am_r.at[slot_index],
+            device_id=where,
+            device_id_type=MESH,
+        )
+
+    am_tp = [send_amax(0, s, at_tp(peer)) for s, peer in enumerate(peers)]
+    am_y = [send_amax(1, 7, at_rep(y_far))]
+    am_z = [send_amax(2, 8, at_rep(z_up)), send_amax(2, 9, at_rep(z_down))]
+    am_w = [send_amax(3, 10, at_rep(z_up))]
+    am_c = [send_amax(4, 11, at_rep(sibling))]
+
+    def fold(copies, index, slots):
+        for copy in copies:
+            copy.wait()
+        total = amax_out[index]
+        for where in slots:
+            total = jnp.maximum(total, amax_in[where])
+        amax_out[index + 1] = total
+
+    for copy in am_tp:
+        copy.start()
+
+    for load in loads[:8]:
+        load.wait()
+
+    def norm(i, carry):
+        rows = pl.ds(pl.multiple_of(i * 32, 32), 32)
+        parts = [rows_in[j, rows, :].astype(F32) for j in range(SPOTS)]
+        square = parts[0] * parts[0]
+        for part in parts[1:]:
+            square = square + part * part
+        mean = jnp.sum(square, axis=1, keepdims=True) / D
+        factor = lax.rsqrt(mean + norm_eps)
+        for j in range(SPOTS):
+            gain = ln_gain[0:1, j * HALF : (j + 1) * HALF]
+            rows_in[j, rows, :] = (parts[j] * factor * gain).astype(BF)
+        return carry
+
+    for copy in a2a[1:4]:
+        copy.wait_recv()
+    send_w(rep, 1, y_far, z_up, z_down, sibling)
+    def beside_first(piece):
+        for dz, target, keep in ((1, z_down, 2), (3, z_up, 3)):
+            block = rep_of(0, dz, 0)
+            arrive_w(block, piece)
+            if piece == keep:
+                send_w(block, piece, target)
+            send_w(block, piece, y_far, sibling)
+
+    beside_first(2)
+    for copy in a2a[4:]:
+        copy.wait_recv()
+    send_w(rep, 0, y_far, z_up, z_down, sibling)
+    beside_first(3)
+    for piece in range(2):
+        send_o(rep, piece, y_far)
+    lax.fori_loop(0, ROWS // 32, norm, 0)
 
     diagonal = lax.broadcasted_iota(jnp.int32, (SEQS, SEQS), 0) == lax.broadcasted_iota(
         jnp.int32, (SEQS, SEQS), 1
@@ -335,6 +359,18 @@
     column = lax.broadcasted_iota(jnp.int32, (1, 768), 1)
     block_of = jnp.right_shift(column * 1366, 16)
     inside = column - block_of * 48
+    plane = jnp.bitwise_and(block_of, 7)
+    off_x = jnp.zeros_like(plane)
+    off_y = jnp.zeros_like(plane)
+    for n, (kx, ky) in enumerate(PLANES):
+        off_x = jnp.where(plane == n, kx, off_x)
+        off_y = jnp.where(plane == n, ky, off_y)
+    block_of = (
+        block_of
+        - plane
+        + jnp.bitwise_and(line_x + 4 - off_x, 3) * 2
+        + jnp.bitwise_and(line_y + off_y, 1)
+    )
     wanted = (
         jnp.where(inside < 40, block_of * SHARD + inside, -1),
         jnp.where(
@@ -351,18 +387,6 @@
             ).astype(BF)
 
     lax.fori_loop(0, STEPS, turn, 0)
-    own_plane.wait()
-    for copy in a2a:
-        copy.wait()
-
-    send_w(rep, 0, y_far)
-    send_w(rep, 1, y_far)
-    send_w(rep, 2, z_up, z_down, sibling)
-    send_w(rep, 3, z_up, z_down, sibling)
-    send_w(rep, 0, z_up, z_down, sibling)
-    send_w(rep, 1, z_up, z_down, sibling)
-    send_w(rep, 2, y_far)
-    send_w(rep, 3, y_far)
 
     acc[...] = jnp.zeros_like(acc)
 
@@ -391,15 +415,8 @@
 
     select(0, 0)
     select(1, 0)
-    for piece in (2, 3):
-        for dz, target, keep in ((1, z_down, 2), (3, z_up, 3)):
-            block = rep_of(0, dz, 0)
-            arrive_w(block, piece)
-            if piece == keep:
-                send_w(block, piece, target)
-            send_w(block, piece, y_far, sibling)
     select(0, 1)
-    for piece in (0, 1):
+    for piece in (1, 0):
         arrive_w(y_far, piece)
         send_w(y_far, piece, z_up, z_down, sibling)
     both_w(0, 0)
@@ -407,7 +424,7 @@
     select(0, 3)
     fold(am_tp, 0, range(7))
     am_y[0].start()
-    for piece in (0, 1):
+    for piece in (1, 0):
         for dz, target, keep in ((1, z_down, 0), (3, z_up, 1)):
             block = rep_of(0, dz, 0)
             arrive_w(block, piece)
@@ -436,7 +453,7 @@
             arrive_w(rep_of(1, dz, 0), piece)
             send_w(rep_of(1, dz, 0), piece, sibling)
     select(0, 2)
-    for piece in (0, 1):
+    for piece in (1, 0):
         for dz, target, keep in ((1, z_down, 0), (3, z_up, 1)):
             block = rep_of(1, dz, 0)
             arrive_w(block, piece)
@@ -448,7 +465,7 @@
     project(1, 1)
     fold(am_z, 2, [8, 9])
     am_w[0].start()
-    for piece in (0, 1):
+    for piece in (1, 0):
         arrive_w(rep_of(0, 2, 0), piece)
         send_w(rep_of(0, 2, 0), piece, sibling)
     far_o()
@@ -459,7 +476,7 @@
     project(0, 2)
     fold(am_w, 3, [10])
     am_c[0].start()
-    for piece in (2, 3, 0, 1):
+    for piece in (2, 3, 1, 0):
         arrive_w(rep_of(1, 2, 0), piece)
         send_w(rep_of(1, 2, 0), piece, sibling)
     both_w(1, 2)
@@ -546,109 +563,198 @@
 
     lax.fori_loop(0, SEQS // 16, attend, 0)
 
-    beside_o(1)
-    for dy in range(2):
-        for dz in (1, 3):
-            both_o(dy, dz)
-
-    lo = pl.ds(0, 256)
-    hi = pl.ds(256, 256)
-
-    def slot_of(index):
-        return rows_in.at[index // 2, pl.ds((index % 2) * 256, 256)]
-
-    def push(index, target):
+    x_up = ((line_x + 1) % 4) * 2 + line_y
+    x_down = ((line_x + 3) % 4) * 2 + line_y
+    y_mate = line_x * 2 + 1 - line_y
+    low, high = (0, LOW), (LOW, ROWS - LOW)
+
+    def push(index, block, rows, spot, target):
         return pltpu.make_async_remote_copy(
-            src_ref=slot_of(index),
-            dst_ref=rs_recv.at[index],
+            src_ref=rows_in.at[block, pl.ds(*rows)],
+            dst_ref=rs_recv.at[spot[0], pl.ds(spot[1], rows[1])],
             send_sem=rs_s.at[index],
             recv_sem=rs_r.at[index],
             device_id=at_tp(target),
             device_id_type=MESH,
         )
 
-    def put(index, values):
-        rows_in[index // 2, pl.ds((index % 2) * 256, 256), :] = values.astype(BF)
-
-    across_x = [((line_x + k) % 4) * 2 + line_y for k in range(4)]
-    y_mate = line_x * 2 + 1 - line_y
-    to_mate = [push(k, y_mate) for k in range(4)]
-    other_x = [push(3 + k, across_x[k]) for k in range(1, 4)]
-    this_hi = [push(6 + k, across_x[k]) for k in range(1, 4)]
-    this_lo = [push(9 + k, across_x[k]) for k in range(1, 4)]
-    last = push(13, y_mate)
+    def line(index, base, spot, rows):
+        half = rows[1] // 2
+        first, second = (rows[0], half), (rows[0] + half, half)
+        return [
+            push(index, base + 2, first, (spot, first[0]), x_up),
+            push(index + 1, base + 2, second, (spot, second[0]), x_down),
+            push(index + 2, base + 1, second, (spot + 1, second[0]), x_up),
+            push(index + 3, base + 1, first, (spot + 1, first[0]), x_up),
+            push(index + 4, base + 3, first, (spot + 2, first[0]), x_down),
+            push(index + 5, base + 3, second, (spot + 2, second[0]), x_down),
+        ]
+
+    to_mate = [push(k, k, low, (4 + k, 0), y_mate) for k in range(4)]
+    other_high = line(4, 0, 4, high)
+    this_high = line(10, 4, 1, high)
+    this_low = line(16, 4, 1, low)
+    last = push(22, 0, high, (7, LOW), y_mate)
+
+    def begin(copies, k):
+        for index in {1: (2,), 2: (0, 1), 3: (4,), 0: ()}[k]:
+            copies[index].start()
+
+    def carry_on(copies, base, spot, rows):
+        half = rows[1] // 2
+        for index, block, first in ((0, 1, rows[0]), (1, 3, rows[0] + half)):
+            copies[index].wait_recv()
+            where = pl.ds(first, half)
+            rows_in[base + block, where, :] = (
+                rows_in[base + block, where, :].astype(F32) + rs_recv[spot, where, :].astype(F32)
+            ).astype(BF)
+            copies[3 if index == 0 else 5].start()
 
     def partial(k, row, rows):
         owner = ((line_x + k) % 4) * 2 + row
         weights = obuf[pl.ds(owner * 2, 2)].reshape(HALF, Q_LOCAL)
         return lax.dot_general(attb[rows, :], weights, nt, preferred_element_type=F32)
 
-    def other_row():
-        for k in (1, 2, 3, 0):
-            put(k, partial(k, 1 - line_y, lo))
-            to_mate[k].start()
-            values = partial(k, 1 - line_y, hi)
-            if k:
-                put(3 + k, values)
-                other_x[k - 1].start()
-            else:
-                own_hi[0] = values
-
-    def this_row():
-        for k in (1, 2, 3, 0):
-            values = partial(k, line_y, hi)
-            if k:
-                put(6 + k, values)
-                this_hi[k - 1].start()
-            else:
-                own_hi[1] = values
-            acc[k // 2, pl.ds((k % 2) * 256, 256), :] = partial(k, line_y, lo)
+    low_rows = slice(0, LOW)
+    high_rows = slice(LOW, ROWS)
+
+    def begin_at(copies, k):
+        if isinstance(k, int):
+            begin(copies, k)
+            return
+        for known in (1, 2, 3):
+            pl.when(k == known)(lambda known=known: begin(copies, known))
+
+    def emit_other(k):
+        rows_in[k, low_rows, :] = partial(k, 1 - line_y, low_rows).astype(BF)
+        push(k, k, low, (4 + k, 0), y_mate).start()
+        rows_in[k, high_rows, :] = partial(k, 1 - line_y, high_rows).astype(BF)
+        begin_at(other_high, k)
+
+    def emit_this(k):
+        rows_in[4 + k, high_rows, :] = partial(k, line_y, high_rows).astype(BF)
+        begin_at(this_high, k)
+        rows_in[4 + k, low_rows, :] = partial(k, line_y, low_rows).astype(BF)
+
+    def pair_at(z_of):
+        k = (z_of // 2 + 4 - line_x) % 4
+        first = 1 + (k + 1) % 2
+        return first, (first + 2) % 4
+
+    near = pair_at(zz)
+    across = pair_at((zz + 2) % 4)
+
+    def from_mate():
+        for k in (2, 1, 3, 0):
+            to_mate[k].wait_recv()
+            rows_in[4 + k, low_rows, :] = (
+                rows_in[4 + k, low_rows, :].astype(F32) + rs_recv[4 + k, low_rows, :].astype(F32)
+            ).astype(BF)
+            begin(this_low, k)
+        carry_on(this_low, 4, 1, low)
 
     other_first = (zz + 1) % 2 == 1 - line_y
-    pl.when(other_first)(other_row)
-    pl.when(jnp.logical_not(other_first))(this_row)
+
+    both_o(0, 0)
+    both_o(1, 0)
+
+    @pl.when(other_first)
+    def _():
+        for k in near:
+            emit_this(k)
+
+    @pl.when(jnp.logical_not(other_first))
+    def _():
+        for k in near:
+            emit_other(k)
+
+    beside_o(1)
+    for dy in range(2):
+        for dz in (1, 3):
+            both_o(dy, dz)
+
+    @pl.when(other_first)
+    def _():
+        for k in (2, 1, 3, 0):
+            emit_other(k)
+        carry_on(other_high, 0, 4, high)
+
+    @pl.when(jnp.logical_not(other_first))
+    def _():
+        for k in (2, 1, 3, 0):
+            emit_this(k)
+        carry_on(this_high, 4, 1, high)
+
     across_o(0)
     across_o(1)
     for dy in range(2):
-        for dz in (0, 2):
-            both_o(dy, dz)
-    pl.when(other_first)(this_row)
-    pl.when(jnp.logical_not(other_first))(other_row)
-
-    for k in (1, 2, 3):
-        to_mate[k].wait_recv()
-        put(9 + k, acc[k // 2, pl.ds((k % 2) * 256, 256), :] + rs_recv[k].astype(F32))
-        this_lo[k - 1].start()
-    for copy in other_x:
-        copy.wait_recv()
-    total = own_hi[0]
-    for k in (1, 2, 3):
-        total = total + rs_recv[3 + k].astype(F32)
-    put(13, total)
-    last.start()
-    to_mate[0].wait_recv()
-
-    def finish(first, gathered, base):
-        def step(i, carry):
-            rows = pl.ds(pl.multiple_of(i * 32, 32), 32)
-            outs = pl.ds(pl.multiple_of(first + i * 32, 32), 32)
-            total = base[rows, :]
-            for index in gathered:
-                total = total + rs_recv[index, rows, :].astype(F32)
-            mixed[outs, :] = (resid[outs, :].astype(F32) + total * scales[3]).astype(BF)
+        both_o(dy, 2)
+
+    @pl.when(other_first)
+    def _():
+        for k in across:
+            emit_this(k)
+        carry_on(this_high, 4, 1, high)
+
+    @pl.when(jnp.logical_not(other_first))
+    def _():
+        for k in across:
+            emit_other(k)
+        carry_on(other_high, 0, 4, high)
+
+    def sum_high():
+        for index in range(2, 6):
+            other_high[index].wait_recv()
+
+        def add_up(i, carry):
+            rows = pl.ds(pl.multiple_of(LOW + i * 32, 32), 32)
+            total = rows_in[0, rows, :].astype(F32)
+            for spot in (5, 6):
+                total = total + rs_recv[spot, rows, :].astype(F32)
+            rows_in[0, rows, :] = total.astype(BF)
             return carry
 
-        lax.fori_loop(0, 8, step, 0)
-
-    for copy in this_lo:
-        copy.wait_recv()
-    finish(0, (0, 10, 11, 12), acc.at[0])
-    for copy in this_hi:
-        copy.wait_recv()
+        lax.fori_loop(0, high[1] // 32, add_up, 0)
+        last.start()
+
+    @pl.when(other_first)
+    def _():
+        sum_high()
+        from_mate()
+
+    @pl.when(jnp.logical_not(other_first))
+    def _():
+        from_mate()
+        sum_high()
+
+    for copies in (this_low, this_high):
+        for index in range(2, 6):
+            copies[index].wait_recv()
+
+    def finish_low(i, carry):
+        rows = pl.ds(pl.multiple_of(i * 32, 32), 32)
+        total = rows_in[4, rows, :].astype(F32)
+        for spot in (2, 3):
+            total = total + rs_recv[spot, rows, :].astype(F32)
+        mixed[rows, :] = (resid[rows, :].astype(F32) + total * scales[3]).astype(BF)
+        return carry
+
+    lax.fori_loop(0, LOW // 32, finish_low, 0)
     last.wait_recv()
-    finish(256, (7, 8, 9, 13), own_hi.at[1])
-
-    for copy in to_mate + other_x + this_hi + this_lo + [last] + sent_w + sent_o:
+
+    def finish_high(i, carry):
+        rows = pl.ds(pl.multiple_of(LOW + i * 32, 32), 32)
+        total = rows_in[4, rows, :].astype(F32)
+        for spot in (2, 3, 7):
+            total = total + rs_recv[spot, rows, :].astype(F32)
+        mixed[rows, :] = (resid[rows, :].astype(F32) + total * scales[3]).astype(BF)
+        return carry
+
+    lax.fori_loop(0, high[1] // 32, finish_high, 0)
+
+    for copy in to_mate + other_high + this_high + this_low + [last]:
+        copy.wait_send()
+    for copy in a2a + sent_w + sent_o:
         copy.wait_send()
     fold(am_c, 4, [11])
     for m in range(4):
@@ -702,9 +808,8 @@
             pltpu.VMEM((2, ROWS, HEAD_DIM), F32),
             pltpu.VMEM((SEQS, 1), F32),
             pltpu.VMEM((2, ROWS, HALF), F32),
-            pltpu.VMEM((2, 256, HALF), F32),
             pltpu.VMEM((ROWS, Q_LOCAL), BF),
-            pltpu.VMEM((14, 256, HALF), BF),
+            pltpu.VMEM((8, ROWS, HALF), BF),
             pltpu.VMEM((ROWS, HALF), BF),
             pltpu.VMEM((6, 8, 128), F32),
             pltpu.VMEM((12, 8, 128), F32),
@@ -715,8 +820,8 @@
             dma((REPS, 4)),
             dma((30,)),
             dma((REPS, 2)),
-            dma((14,)),
-            dma((14,)),
+            dma((23,)),
+            dma((23,)),
             dma((12,)),
             dma((12,)),
         ],

time: 149 us -> 139 us (0.933)
  Pallas kernels: 145 us -> 134 us
    pallas_call x1, Pallas kernels: 145 us -> 134 us  [shards(): pl.pallas_call(kernel, out_shape=(jax.ShapeDtypeStruct((ROWS, HALF), BF),...]
where the time goes in v3:
time: 139 us; the launch traced here: 138 us
  Pallas kernels  134 us (96%)
  local copies, waits for them, and re-layouts  3.23 us (2%)
    pallas_call x1, Pallas kernels, shards(): pl.pallas_call(kernel, out_shape=(jax.ShapeDtypeStruct((ROWS, HALF), BF),...  134 us
    unnamed x2, local copies, waits for them, and re-layouts  3.23 us

profile of v3, /device:TPU:1, one launch (start us, length us, event | category | flops | bytes accessed | tf_op | source)
XLA Modules:
  0.0 138.1 jit_solution(6857138956746499406)
XLA Ops:
  0.6 134.2 %shard_map.149 = (bf16[512,640]{1,0:T(8,128)(2,1)}, f32[4,16]{1,0:T(4,128)}) custom-call(bf16[512,5120]{1,0:T(8,128)(2,1)} %bitcast.8, f32[1,5120]{1,0:T(1,128)} %bitcast.10, f32[1,128]{1,0:T(1,128)} %bitcast.11, f32[1,128]{1,0:T(1,128)} %bitcast.12, bf16[40,8192]{1,0:T(8,128)(2,1)} %w_query.1, bf16[40,1024]{1,0:T(8,128)(2,1)} %w_key.1, ...), custom_call_target="tpu_custom_call" | custom-call | flops 12999999488 | bytes 13000000 | tf_op jit(solution)/shard_map/pallas_call | solution.py:790
  134.8 2.0 %copy.18 = bf16[4,128,640]{2,1,0:T(8,128)(2,1)} copy(bf16[4,128,640]{2,1,0:T(8,128)(2,1)} %bitcast.7) | data formatting | bytes 1310720
  136.8 1.2 copy.19

commit v4 on v3

--- a/solution.py
+++ b/solution.py
@@ -468,8 +468,6 @@
     for piece in (1, 0):
         arrive_w(rep_of(0, 2, 0), piece)
         send_w(rep_of(0, 2, 0), piece, sibling)
-    far_o()
-    beside_o(0)
     both_w(1, 3)
     project(1, 3)
     both_w(0, 2)
@@ -479,6 +477,8 @@
     for piece in (2, 3, 1, 0):
         arrive_w(rep_of(1, 2, 0), piece)
         send_w(rep_of(1, 2, 0), piece, sibling)
+    far_o()
+    beside_o(0)
     both_w(1, 2)
     project(1, 2)
 

time: 139 us -> 138 us (level)
  no operation moved by 1% of the time
where the time goes in v4:
time: 138 us; the launch traced here: 137 us
  Pallas kernels  133 us (96%)
  local copies, waits for them, and re-layouts  3.23 us (2%)
    pallas_call x1, Pallas kernels, shards(): pl.pallas_call(kernel, out_shape=(jax.ShapeDtypeStruct((ROWS, HALF), BF),...  133 us
    unnamed x2, local copies, waits for them, and re-layouts  3.23 us

profile of v4, /device:TPU:1, one launch (start us, length us, event | category | flops | bytes accessed | tf_op | source)
XLA Modules:
  0.0 137.3 jit_solution(747891920674060717)
XLA Ops:
  0.6 133.4 %shard_map.149 = (bf16[512,640]{1,0:T(8,128)(2,1)}, f32[4,16]{1,0:T(4,128)}) custom-call(bf16[512,5120]{1,0:T(8,128)(2,1)} %bitcast.8, f32[1,5120]{1,0:T(1,128)} %bitcast.10, f32[1,128]{1,0:T(1,128)} %bitcast.11, f32[1,128]{1,0:T(1,128)} %bitcast.12, bf16[40,8192]{1,0:T(8,128)(2,1)} %w_query.1, bf16[40,1024]{1,0:T(8,128)(2,1)} %w_key.1, ...), custom_call_target="tpu_custom_call" | custom-call | flops 12999999488 | bytes 13000000 | tf_op jit(solution)/shard_map/pallas_call | solution.py:790
  134.1 2.0 %copy.18 = bf16[4,128,640]{2,1,0:T(8,128)(2,1)} copy(bf16[4,128,640]{2,1,0:T(8,128)(2,1)} %bitcast.7) | data formatting | bytes 1310720
  136.0 1.2 copy.19
